TPU v7x, 128 devices: a whole 4x4x4 slice. The times are simulated.
128 devices in a mesh: dp: 8 (over y, core), fsdp: 16 (over z, x).
Axes of the slice: x: 4, y: 4, z: 4, core: 2. Of those that a mesh axis runs over, the one named last changes fastest.
Arguments:
- data_samples: bfloat16 [1024, 4096], P('dp', 'fsdp'), may hold values from -6 to 6
- negative_start: float32 [1024, 4096], P('dp', 'fsdp'), may hold values from -6 to 6
- langevin_noise: float32 [4, 1024, 4096], P(None, 'dp', 'fsdp'), may hold values from -6 to 6
- first_weight: bfloat16 [4096, 4096], P('fsdp'), may hold values from -0.09375 to 0.09375
- second_weight: bfloat16 [4096, 4096], P('fsdp'), may hold values from -0.09375 to 0.09375
- readout: float32 [4096], P('fsdp'), may hold values from -480 to 480
Outputs:
- first_grad: float32 [4096, 4096], P('fsdp', 'dp')
- second_grad: float32 [4096, 4096], P('fsdp', 'dp')
- energy_gap: float32 [], replicated
All inputs are finite; a program needn't handle non-finite values.
Results may differ from a plain program's by a relative error of at most 0.014.
Values may be sent and summed in bfloat16 or wider, within the bound.
No kernel may reach another device: no remote copies, remote signals or barrier semaphores. Data moves between devices by JAX's collectives and lax.ppermute only.
A program may use at most 64 MiB of HBM per device.

v0:
```python
import functools

import jax
import jax.numpy as jnp
from jax import lax
from jax.sharding import Mesh
from jax.sharding import PartitionSpec as P

D = 4096
H = 4096
STEPS = 4
FSDP = ("fsdp_0", "fsdp_1")
DP = ("dp_0", "dp_1")
DP_FSDP = ("dp_0", "dp_1", "fsdp_0", "fsdp_1")


def split_up(value, dim, length):
    before, after = (value.shape[:dim], value.shape[dim + 1 :])
    return jnp.moveaxis(value.reshape(*before, length, -1, *after), dim, 0)


def sum_at_owner(value, axis, dim):
    length = lax.axis_size(axis)
    parts = lax.all_to_all(split_up(value, dim, length), axis, 0, 0, tiled=True)
    return jnp.sum(parts.astype(jnp.float32), axis=0)


def in_order(parts, dim):
    parts = jnp.moveaxis(parts, 0, dim)
    lengths = parts.shape
    return parts.reshape(*lengths[:dim], lengths[dim] * lengths[dim + 1], *lengths[dim + 2 :])


def copy_for_each(value, axis):
    copies = jnp.broadcast_to(value, (lax.axis_size(axis), *value.shape))
    return lax.all_to_all(copies, axis, split_axis=0, concat_axis=0, tiled=True)


def collect(value, axis, dim):
    return in_order(copy_for_each(value, axis), dim)


def sent_together(arrays, axis, dim, along):
    ends, at = ([], 0)
    for a in arrays[:-1]:
        at += a.shape[along]
        ends.append(at)
    both = jnp.concatenate(arrays, axis=along)
    return tuple(
        jnp.split(lax.psum_scatter(both, axis, scatter_dimension=dim, tiled=True), ends, axis=along)
    )


def over_axes(value, axes):
    return functools.reduce(lax.psum, axes, value)


def slope(values):
    sig = jax.nn.sigmoid(values)
    return sig * (1.0 + values * (1.0 - sig))


def forward(inputs, first_weight, second_weight):
    term_one = jnp.dot(inputs, first_weight, preferred_element_type=jnp.float32)
    pre_one = sum_at_owner(term_one.astype(jnp.bfloat16), FSDP, 1)
    hidden = jax.nn.silu(pre_one).astype(jnp.bfloat16)
    term_two = jnp.dot(hidden, second_weight, preferred_element_type=jnp.float32)
    pre_two = sum_at_owner(term_two.astype(jnp.bfloat16), FSDP, 1)
    return (pre_one, hidden, pre_two)


def backward(cotan, readout, pre_one, pre_two, second_weight):
    grad_two = (cotan[:, None] * readout[None, :] * slope(pre_two)).astype(jnp.bfloat16)
    full_two = collect(grad_two, FSDP, 1)
    back_one = lax.dot_general(
        full_two, second_weight, (((1,), (1,)), ((), ())), preferred_element_type=jnp.float32
    )
    grad_one = (back_one * slope(pre_one)).astype(jnp.bfloat16)
    full_one = collect(grad_one, FSDP, 1)
    return (full_two, full_one)


def contract_rows(left, right):
    return lax.dot_general(
        left, right, (((0,), (0,)), ((), ())), preferred_element_type=jnp.float32
    )


def one_pass(inputs, cotan, readout, first_weight, second_weight):
    pre_one, hidden, pre_two = forward(inputs, first_weight, second_weight)
    energies = jnp.dot(jax.nn.silu(pre_two), readout, precision=lax.Precision.HIGHEST)
    full_two, full_one = backward(cotan, readout, pre_one, pre_two, second_weight)
    raw_one = contract_rows(inputs, full_one)
    raw_two = contract_rows(hidden, full_two)
    return (jnp.sum(cotan * energies), raw_one, raw_two)


def local(data_samples, negative_start, langevin_noise, first_weight, second_weight, readout):
    state = negative_start
    ones = jnp.ones((state.shape[0],), jnp.float32)
    for step in range(STEPS):
        inputs = state.astype(jnp.bfloat16)
        pre_one, hidden, pre_two = forward(inputs, first_weight, second_weight)
        full_two, full_one = backward(ones, readout, pre_one, pre_two, second_weight)
        moved = lax.dot_general(
            full_one, first_weight, (((1,), (1,)), ((), ())), preferred_element_type=jnp.float32
        )
        state = state - 0.005 * moved + 0.1 * langevin_noise[step]
    negatives = state.astype(jnp.bfloat16)
    rows = jnp.concatenate([data_samples, negatives], axis=0)
    cotan = jnp.concatenate([ones, -ones])
    signed, raw_one, raw_two = one_pass(rows, cotan, readout, first_weight, second_weight)
    group_one, group_two = sent_together((raw_one, raw_two), DP, 1, 0)
    squares = jnp.sum(group_one * group_one) + jnp.sum(group_two * group_two)
    signed_total = over_axes(signed, DP_FSDP)
    square_total = over_axes(squares, DP_FSDP)
    energy_gap = signed_total / (
        state.shape[0] * lax.axis_size(DP) * 80.0 * jnp.sqrt(jnp.float32(H))
    )
    scale = jnp.sqrt(square_total / (2.0 * D * H) + 1e-06)
    return (group_one / scale, group_two / scale, energy_gap)


def solution(mesh):
    split = Mesh(mesh.devices.reshape(4, 2, 4, 4), ("dp_0", "dp_1", "fsdp_0", "fsdp_1"))
    in_specs = (P(DP, FSDP), P(DP, FSDP), P(None, DP, FSDP), P(FSDP, None), P(FSDP, None), P(FSDP))
    out_specs = (P(FSDP, DP), P(FSDP, DP), P())
    return jax.shard_map(local, mesh=split, in_specs=in_specs, out_specs=out_specs, check_vma=False)
```

profile of v0, /device:TPU:0, one launch (start us, length us, event | category | flops | bytes accessed | tf_op | source)
XLA Modules:
  0.0 557.8 jit_solution(8974331041981539300)
XLA Ops:
  7.2 2.2 convolution_convert_fusion.9
  9.5 24.9 %all_to_all.100 = bf16[16,128,256]{2,1,0:T(8,128)(2,1)S(1)} all-to-all(bf16[16,128,256]{2,1,0:T(8,128)(2,1)S(1)} %bitcast.159), channel_id=1, replica_groups=mesh['dp_0'=4,'dp_1'=2,'fsdp_0'=4,'fsdp_1'=4] {'fsdp_0','fsdp_1'}, dimensions={0} | all-to-all | bytes 2097152 | tf_op jit(solution)/shard_map/all_to_all | solution.py:24
  35.2 19.3 %all_to_all.101 = bf16[16,128,256]{2,1,0:T(8,128)(2,1)S(1)} all-to-all(bf16[16,128,256]{2,1,0:T(8,128)(2,1)S(1)} %bitcast.160), channel_id=1, replica_groups=mesh['dp_0'=4,'dp_1'=2,'fsdp_0'=4,'fsdp_1'=4] {'fsdp_0','fsdp_1'}, dimensions={0} | all-to-all | bytes 2097152 | tf_op jit(solution)/shard_map/all_to_all | solution.py:24
  55.1 18.1 %all_to_all.102 = bf16[16,128,256]{1,2,0:T(8,128)(2,1)S(1)} all-to-all(bf16[16,128,256]{1,2,0:T(8,128)(2,1)S(1)} %broadcast_in_dim.35), channel_id=1, replica_groups=mesh['dp_0'=4,'dp_1'=2,'fsdp_0'=4,'fsdp_1'=4] {'fsdp_0','fsdp_1'}, dimensions={0} | all-to-all | bytes 2097152 | tf_op jit(solution)/shard_map/all_to_all | solution.py:36
  74.4 17.0 %all_to_all.103 = bf16[16,128,256]{1,2,0:T(8,128)(2,1)S(1)} all-to-all(bf16[16,128,256]{1,2,0:T(8,128)(2,1)S(1)} %broadcast_in_dim.36), channel_id=1, replica_groups=mesh['dp_0'=4,'dp_1'=2,'fsdp_0'=4,'fsdp_1'=4] {'fsdp_0','fsdp_1'}, dimensions={0} | all-to-all | bytes 2097152 | tf_op jit(solution)/shard_map/all_to_all | solution.py:36
  92.8 16.1 %all_to_all.104 = bf16[16,128,256]{2,1,0:T(8,128)(2,1)S(1)} all-to-all(bf16[16,128,256]{2,1,0:T(8,128)(2,1)S(1)} %bitcast.161), channel_id=1, replica_groups=mesh['dp_0'=4,'dp_1'=2,'fsdp_0'=4,'fsdp_1'=4] {'fsdp_0','fsdp_1'}, dimensions={0} | all-to-all | bytes 2097152 | tf_op jit(solution)/shard_map/all_to_all | solution.py:24
  109.6 15.9 %all_to_all.105 = bf16[16,128,256]{2,1,0:T(8,128)(2,1)S(1)} all-to-all(bf16[16,128,256]{2,1,0:T(8,128)(2,1)S(1)} %bitcast.162), channel_id=1, replica_groups=mesh['dp_0'=4,'dp_1'=2,'fsdp_0'=4,'fsdp_1'=4] {'fsdp_0','fsdp_1'}, dimensions={0} | all-to-all | bytes 2097152 | tf_op jit(solution)/shard_map/all_to_all | solution.py:24
  126.0 15.9 %all_to_all.106 = bf16[16,128,256]{1,2,0:T(8,128)(2,1)S(1)} all-to-all(bf16[16,128,256]{1,2,0:T(8,128)(2,1)S(1)} %broadcast_in_dim.37), channel_id=1, replica_groups=mesh['dp_0'=4,'dp_1'=2,'fsdp_0'=4,'fsdp_1'=4] {'fsdp_0','fsdp_1'}, dimensions={0} | all-to-all | bytes 2097152 | tf_op jit(solution)/shard_map/all_to_all | solution.py:36
  143.1 16.1 %all_to_all.107 = bf16[16,128,256]{1,2,0:T(8,128)(2,1)S(1)} all-to-all(bf16[16,128,256]{1,2,0:T(8,128)(2,1)S(1)} %broadcast_in_dim.38), channel_id=1, replica_groups=mesh['dp_0'=4,'dp_1'=2,'fsdp_0'=4,'fsdp_1'=4] {'fsdp_0','fsdp_1'}, dimensions={0} | all-to-all | bytes 2097152 | tf_op jit(solution)/shard_map/all_to_all | solution.py:36
  160.6 17.1 %all_to_all.108 = bf16[16,128,256]{2,1,0:T(8,128)(2,1)S(1)} all-to-all(bf16[16,128,256]{2,1,0:T(8,128)(2,1)S(1)} %bitcast.163), channel_id=1, replica_groups=mesh['dp_0'=4,'dp_1'=2,'fsdp_0'=4,'fsdp_1'=4] {'fsdp_0','fsdp_1'}, dimensions={0} | all-to-all | bytes 2097152 | tf_op jit(solution)/shard_map/all_to_all | solution.py:24
  178.4 19.6 %all_to_all.109 = bf16[16,128,256]{2,1,0:T(8,128)(2,1)S(1)} all-to-all(bf16[16,128,256]{2,1,0:T(8,128)(2,1)S(1)} %bitcast.164), channel_id=1, replica_groups=mesh['dp_0'=4,'dp_1'=2,'fsdp_0'=4,'fsdp_1'=4] {'fsdp_0','fsdp_1'}, dimensions={0} | all-to-all | bytes 2097152 | tf_op jit(solution)/shard_map/all_to_all | solution.py:24
  198.6 19.4 %all_to_all.110 = bf16[16,128,256]{1,2,0:T(8,128)(2,1)S(1)} all-to-all(bf16[16,128,256]{1,2,0:T(8,128)(2,1)S(1)} %broadcast_in_dim.39), channel_id=1, replica_groups=mesh['dp_0'=4,'dp_1'=2,'fsdp_0'=4,'fsdp_1'=4] {'fsdp_0','fsdp_1'}, dimensions={0} | all-to-all | bytes 2097152 | tf_op jit(solution)/shard_map/all_to_all | solution.py:36
  219.2 21.7 %all_to_all.111 = bf16[16,128,256]{1,2,0:T(8,128)(2,1)S(1)} all-to-all(bf16[16,128,256]{1,2,0:T(8,128)(2,1)S(1)} %broadcast_in_dim.40), channel_id=1, replica_groups=mesh['dp_0'=4,'dp_1'=2,'fsdp_0'=4,'fsdp_1'=4] {'fsdp_0','fsdp_1'}, dimensions={0} | all-to-all | bytes 2097152 | tf_op jit(solution)/shard_map/all_to_all | solution.py:36
  242.4 19.8 %all_to_all.112 = bf16[16,128,256]{2,1,0:T(8,128)(2,1)S(1)} all-to-all(bf16[16,128,256]{2,1,0:T(8,128)(2,1)S(1)} %bitcast.165), channel_id=1, replica_groups=mesh['dp_0'=4,'dp_1'=2,'fsdp_0'=4,'fsdp_1'=4] {'fsdp_0','fsdp_1'}, dimensions={0} | all-to-all | bytes 2097152 | tf_op jit(solution)/shard_map/all_to_all | solution.py:24
  262.9 18.4 %all_to_all.113 = bf16[16,128,256]{2,1,0:T(8,128)(2,1)S(1)} all-to-all(bf16[16,128,256]{2,1,0:T(8,128)(2,1)S(1)} %bitcast.166), channel_id=1, replica_groups=mesh['dp_0'=4,'dp_1'=2,'fsdp_0'=4,'fsdp_1'=4] {'fsdp_0','fsdp_1'}, dimensions={0} | all-to-all | bytes 2097152 | tf_op jit(solution)/shard_map/all_to_all | solution.py:24
  281.8 18.0 %all_to_all.114 = bf16[16,128,256]{1,2,0:T(8,128)(2,1)S(1)} all-to-all(bf16[16,128,256]{1,2,0:T(8,128)(2,1)S(1)} %broadcast_in_dim.41), channel_id=1, replica_groups=mesh['dp_0'=4,'dp_1'=2,'fsdp_0'=4,'fsdp_1'=4] {'fsdp_0','fsdp_1'}, dimensions={0} | all-to-all | bytes 2097152 | tf_op jit(solution)/shard_map/all_to_all | solution.py:36
  301.0 21.6 %all_to_all.115 = bf16[16,128,256]{1,2,0:T(8,128)(2,1)S(1)} all-to-all(bf16[16,128,256]{1,2,0:T(8,128)(2,1)S(1)} %broadcast_in_dim.42), channel_id=1, replica_groups=mesh['dp_0'=4,'dp_1'=2,'fsdp_0'=4,'fsdp_1'=4] {'fsdp_0','fsdp_1'}, dimensions={0} | all-to-all | bytes 2097152 | tf_op jit(solution)/shard_map/all_to_all | solution.py:36
  324.4 32.1 %all_to_all.116 = bf16[16,256,256]{2,1,0:T(8,128)(2,1)S(1)} all-to-all(bf16[16,256,256]{2,1,0:T(8,128)(2,1)S(1)} %bitcast.143), channel_id=1, replica_groups=mesh['dp_0'=4,'dp_1'=2,'fsdp_0'=4,'fsdp_1'=4] {'fsdp_0','fsdp_1'}, dimensions={0} | all-to-all | bytes 4194304 | tf_op jit(solution)/shard_map/all_to_all | solution.py:24
  357.8 30.8 %all_to_all.117 = bf16[16,256,256]{2,1,0:T(8,128)(2,1)S(1)} all-to-all(bf16[16,256,256]{2,1,0:T(8,128)(2,1)S(1)} %bitcast.144), channel_id=1, replica_groups=mesh['dp_0'=4,'dp_1'=2,'fsdp_0'=4,'fsdp_1'=4] {'fsdp_0','fsdp_1'}, dimensions={0} | all-to-all | bytes 4194304 | tf_op jit(solution)/shard_map/all_to_all | solution.py:24
  389.7 32.7 %all_to_all.118 = bf16[16,256,256]{1,2,0:T(8,128)(2,1)S(1)} all-to-all(bf16[16,256,256]{1,2,0:T(8,128)(2,1)S(1)} %broadcast_in_dim.43), channel_id=1, replica_groups=mesh['dp_0'=4,'dp_1'=2,'fsdp_0'=4,'fsdp_1'=4] {'fsdp_0','fsdp_1'}, dimensions={0} | all-to-all | bytes 4194304 | tf_op jit(solution)/shard_map/all_to_all | solution.py:36
  426.2 4.4 all-to-all-start.19
  430.7 4.3 fusion.33
  435.0 16.6 %all-to-all-done.19 = bf16[16,256,256]{1,2,0:T(8,128)(2,1)} async-done(((bf16[16,256,256]{1,2,0:T(8,128)(2,1)}), bf16[16,256,256]{1,2,0:T(8,128)(2,1)}, u32[]{:S(2)}, u32[]{:S(2)}) %all-to-all-start.19) | async-done | bytes 2097184 | tf_op jit(solution)/shard_map/all_to_all | solution.py:36
  451.6 2.5 fusion.17
  454.5 3.8 pad_maximum_fusion
  459.2 49.2 %reduce-scatter.2.cloned.1.call-done = f32[512,512]{1,0:T(8,128)} async-done(((f32[512,4096]{1,0:T(8,128)}), f32[512,512]{1,0:T(8,128)}) %reduce-scatter.2.cloned.1.call-update) | async-done | bytes 1048592 | tf_op jit(solution)/shard_map/reduce_scatter | solution.py:50
  508.4 1.9 multiply_reduce_fusion
  511.6 9.2 %all-reduce.2 = (f32[]{:T(128)}, f32[]{:T(128)}) all-reduce(f32[]{:T(128)S(6)} %add.128, f32[]{:T(128)} %multiply_reduce_fusion.2), channel_id=1, replica_groups=mesh['dp_0'=4,'dp_1'=2,'fsdp_0'=4,'fsdp_1'=4] {'dp_0'}, use_global_device_ids=true, to_apply=%region_13.14 | all-reduce | flops 2 | bytes 16 | tf_op jit(solution)/shard_map/psum | solution.py:55
  520.8 3.1 all-reduce.3
  523.9 11.3 %all-reduce.1 = (f32[]{:T(128)}, f32[]{:T(128)}) all-reduce(f32[]{:T(128)} %get-tuple-element.11, f32[]{:T(128)} %get-tuple-element.12), channel_id=1, replica_groups=mesh['dp_0'=4,'dp_1'=2,'fsdp_0'=4,'fsdp_1'=4] {'fsdp_0'}, use_global_device_ids=true, to_apply=%region_15.16 | all-reduce | flops 2 | bytes 16 | tf_op jit(solution)/shard_map/psum | solution.py:55
  535.2 11.0 %all-reduce = (f32[]{:T(128)}, f32[]{:T(128)}) all-reduce(f32[]{:T(128)} %get-tuple-element.7, f32[]{:T(128)} %get-tuple-element.8), channel_id=1, replica_groups=mesh['dp_0'=4,'dp_1'=2,'fsdp_0'=4,'fsdp_1'=4] {'fsdp_1'}, use_global_device_ids=true, to_apply=%region_16.17 | all-reduce | flops 2 | bytes 16 | tf_op jit(solution)/shard_map/psum | solution.py:55
  547.6 2.3 slice_divide_fusion
  (91 shorter events, 23.0 us)
Async XLA Ops:
  7.2 27.4 %copy-start = (bf16[256,4096]{1,0:T(8,128)(2,1)S(1)}, bf16[256,4096]{1,0:T(8,128)(2,1)}, u32[]{:S(2)}) copy-start(bf16[256,4096]{1,0:T(8,128)(2,1)} %param.10) | copy-start | bytes 6291460
  35.2 19.5 %copy-start.10 = (f32[256]{0:T(256)S(1)}, f32[256]{0:T(256)}, u32[]{:S(2)}) copy-start(f32[256]{0:T(256)} %param.11) | copy-start | bytes 3076
  74.0 17.3 %copy-start.7 = (f32[4,128,256]{2,1,0:T(8,128)S(1)}, f32[4,128,256]{2,1,0:T(8,128)}, u32[]{:S(2)}) copy-start(f32[4,128,256]{2,1,0:T(8,128)} %param.8) | copy-start | bytes 1572868
  74.1 17.3 %copy-start.8 = (f32[128,256]{1,0:T(8,128)S(1)}, f32[128,256]{1,0:T(8,128)}, u32[]{:S(2)}) copy-start(f32[128,256]{1,0:T(8,128)} %param.7) | copy-start | bytes 393220
  74.2 17.2 %copy-start.1 = (bf16[256,4096]{1,0:T(8,128)(2,1)S(1)}, bf16[256,4096]{1,0:T(8,128)(2,1)}, u32[]{:S(2)}) copy-start(bf16[256,4096]{1,0:T(8,128)(2,1)} %param.9) | copy-start | bytes 6291460
  142.9 16.3 %copy-start.2 = (bf16[256,4096]{1,0:T(8,128)(2,1)S(1)}, bf16[256,4096]{1,0:T(8,128)(2,1)}, u32[]{:S(2)}) copy-start(bf16[256,4096]{1,0:T(8,128)(2,1)} %param.9) | copy-start | bytes 6291460
  219.0 22.0 %copy-start.3 = (bf16[256,4096]{1,0:T(8,128)(2,1)S(1)}, bf16[256,4096]{1,0:T(8,128)(2,1)}, u32[]{:S(2)}) copy-start(bf16[256,4096]{1,0:T(8,128)(2,1)} %param.9) | copy-start | bytes 6291460
  300.8 21.8 %copy-start.4 = (bf16[256,4096]{1,0:T(8,128)(2,1)S(1)}, bf16[256,4096]{1,0:T(8,128)(2,1)}, u32[]{:S(2)}) copy-start(bf16[256,4096]{1,0:T(8,128)(2,1)} %param.9) | copy-start | bytes 6291460
  322.6 0.9 copy-start.9
  388.6 0.7 copy-start.11
  422.4 1.3 copy-start.6
  426.2 25.4 %all-to-all-start.19 = ((bf16[16,256,256]{1,2,0:T(8,128)(2,1)}), bf16[16,256,256]{1,2,0:T(8,128)(2,1)}, u32[]{:S(2)}, u32[]{:S(2)}) async-start(bf16[16,256,256]{1,2,0:T(8,128)(2,1)} %broadcast_in_dim.44), calls=%async_computation.19 | async-start | bytes 4194304 | tf_op jit(solution)/shard_map/all_to_all | solution.py:36
  430.7 77.7 %reduce-scatter.2.cloned.1.call-start = ((), (), s32[]{:S(2)}) async-start(), calls=%async_computation.21 | async-start | bytes 9437184 | tf_op jit(solution)/shard_map/reduce_scatter | solution.py:50
  451.6 2.8 copy-start.5
Sparse Core Ops, SparseCore 0:
  458.4 49.9 reduce-scatter.1
where the time goes:
time: 559 us; the launch traced here: 558 us
  blocking collectives  429 us (77%)
  waiting for transfers between devices  65.8 us (12%)
  matrix products  21.5 us (4%)
  between operations  18.3 us (3%)
  other arithmetic  10.7 us (2%)
  local copies, waits for them, and re-layouts  7.75 us (1%)
    all_to_all x10, blocking collectives, sum_at_owner(): parts = lax.all_to_all(split_up(value, dim, length), axis, 0, 0, tiled=True)  214 us
    all_to_all x9, blocking collectives, copy_for_each(): return lax.all_to_all(copies, axis, split_axis=0, concat_axis=0, tiled=True)  181 us
    reduce_scatter x1, waiting for transfers between devices, sent_together(): lax.psum_scatter(both, axis, scatter_dimension=dim, tiled=True)  49.2 us
    psum x4, blocking collectives, over_axes(): return functools.reduce(lax.psum, axes, value)  34.6 us
    all_to_all x1, waiting for transfers between devices, copy_for_each(): return lax.all_to_all(copies, axis, split_axis=0, concat_axis=0, tiled=True)  16.6 us
  transfers between devices with their start and end apart: 2, of which 2 were waited for; matrix products, arithmetic and copies ran while one was open for 1% of the time, Pallas kernels for 0%

commit v1 on v0

v1 whole, which is shorter than its diff:
```python
import jax
import jax.numpy as jnp
from jax import lax
from jax.sharding import Mesh
from jax.sharding import PartitionSpec as P

STEPS = 4
AXES = ("y", "c", "z", "a", "b")
DP = ("y", "c")
ZA = ("z", "a")
FSDP = ("z", "a", "b")
SWAP = [(0, 1), (1, 0)]
UP = [(0, 1), (1, 2), (2, 3), (3, 0)]
DOWN = [(0, 3), (1, 0), (2, 1), (3, 2)]
OVER = [(0, 2), (1, 3), (2, 0), (3, 1)]


def pick(value, index, dim):
    return lax.dynamic_index_in_dim(value, index, dim, keepdims=False)


def swap(value, axis):
    return lax.ppermute(value, axis, SWAP)


def put(buffer, piece, starts):
    starts = tuple(starts) + (0,) * (buffer.ndim - len(starts))
    return lax.dynamic_update_slice(buffer, piece, starts)


def ring_bulk(piece, axis):
    half = piece.shape[-2] // 2
    from_low = lax.ppermute(piece, axis, UP)
    from_high = lax.ppermute(piece, axis, DOWN)
    far_a = lax.ppermute(from_low[..., :half, :], axis, UP)
    far_b = lax.ppermute(from_high[..., half:, :], axis, DOWN)
    far = jnp.concatenate([far_a, far_b], axis=-2)
    return (piece, from_low, from_high, far)


def ring_order(axis):
    me = lax.axis_index(axis)
    return (me, (me + 3) % 4, (me + 1) % 4, (me + 2) % 4)


def gather_first(weight, c, b):
    rows, cols = weight.shape
    unit = cols // 16
    a = lax.axis_index("a")
    piece = pick(weight.reshape(rows, 8, 2, unit), c, 2).reshape(rows, 8 * unit)
    across = swap(piece, "a")
    out = jnp.zeros((4, 2, rows, 8 * unit), weight.dtype)
    for value, at in ((piece, a), (across, 1 - a)):
        for part, z in zip(ring_bulk(value, "z"), ring_order("z")):
            out = put(out, part[None, None], (z, at))
    return out.reshape(8, rows, 8 * unit)


def gather_second(weight, c, b):
    rows, cols = weight.shape
    unit = cols // 16
    part = rows // 4
    y, a = lax.axis_index("y"), lax.axis_index("a")
    mine = lax.dynamic_slice_in_dim(weight, y * part, part, 0).reshape(part, 8, 2, unit)
    theirs = swap(pick(mine, 1 - b, 2), "b")
    piece = jnp.where(c == b, pick(mine, b, 2), theirs).reshape(part, 8 * unit)
    across = swap(piece, "a")
    both = jnp.where(a == 0, jnp.stack([piece, across]), jnp.stack([across, piece]))
    column = jnp.zeros((4, 2, part, 8 * unit), weight.dtype)
    moves = (both, *(lax.ppermute(both, "z", way) for way in (UP, DOWN, OVER)))
    for value, z in zip(moves, ring_order("z")):
        column = put(column, value[None], (z,))
    out = jnp.zeros((4, 2, 4, part, 8 * unit), weight.dtype)
    for value, at in zip(ring_bulk(column, "y"), ring_order("y")):
        out = put(out, value[:, :, None], (0, 0, at))
    return out.reshape(8, rows, 8 * unit)


def to_groups(value):
    lead, rows, cols = value.shape
    part = rows // 8
    split = jnp.moveaxis(value.reshape(lead, 8, part, cols), 1, 0)
    got = lax.all_to_all(split, ZA, 0, 0, tiled=True)
    own = jnp.transpose(got, (1, 2, 0, 3)).reshape(lead, part, 8 * cols)
    other = swap(own, "c")
    first = lax.axis_index("c") == 0
    return jnp.concatenate([jnp.where(first, own, other), jnp.where(first, other, own)], axis=1)


def spread(value, axis):
    count = lax.axis_size(axis)
    return lax.all_to_all(jnp.broadcast_to(value, (count, *value.shape)), axis, 0, 0, tiled=True)


def slope(values):
    sig = jax.nn.sigmoid(values)
    return sig * (1.0 + values * (1.0 - sig))


def share(part, axis):
    return part + swap(part, axis)


def layer(inputs, block, axis):
    slices, depth, _ = block.shape
    split = inputs.reshape(inputs.shape[0], slices, depth)
    terms = jnp.einsum("rnk,nkm->nrm", split, block, preferred_element_type=jnp.float32)
    part = jnp.sum(terms.astype(jnp.bfloat16).astype(jnp.float32), axis=0)
    return share(part, axis)


def back(cotan, block, axis):
    flat = block.reshape(-1, block.shape[-1])
    part = lax.dot_general(
        cotan, flat, (((1,), (1,)), ((), ())), preferred_element_type=jnp.float32
    )
    return share(part, axis)


def one_pass(inputs, cotan, readout, first, second):
    pre_one = layer(inputs, first, "b")
    hidden = jax.nn.silu(pre_one).astype(jnp.bfloat16)
    pre_two = layer(hidden, second, "c")
    grad_two = (cotan[:, None] * readout[None, :] * slope(pre_two)).astype(jnp.bfloat16)
    grad_one = (back(grad_two, second, "b") * slope(pre_one)).astype(jnp.bfloat16)
    return (hidden, pre_two, grad_two, grad_one)


def local(data_samples, negative_start, langevin_noise, first_weight, second_weight, readout):
    c, b = lax.axis_index("c"), lax.axis_index("b")
    first = gather_first(first_weight, c, b)
    second = gather_second(second_weight, c, b)
    moved_in = to_groups(jnp.concatenate([negative_start[None], langevin_noise]))
    data = to_groups(data_samples[None])[0]
    state, noise = (moved_in[0], moved_in[1:])
    readout = spread(readout, ZA).reshape(-1)
    count = state.shape[0]
    ones = jnp.ones((count,), jnp.float32)
    for step in range(STEPS):
        inputs = state.astype(jnp.bfloat16)
        _, _, _, grad_one = one_pass(inputs, ones, readout, first, second)
        state = state - 0.005 * back(grad_one, first, "c") + 0.1 * noise[step]
    rows = jnp.concatenate([data, state.astype(jnp.bfloat16)], axis=0)
    cotan = jnp.concatenate([ones, -ones])
    hidden, pre_two, grad_two, grad_one = one_pass(rows, cotan, readout, first, second)
    energies = jnp.sum(jax.nn.silu(pre_two) * readout[None, :], axis=1)
    signed = 0.5 * jnp.sum(cotan * energies)

    unit = rows.shape[1] // 8
    half = lambda value, at: pick(value.reshape(2, count, 8, unit), at, 0)
    crossed = swap(half(hidden, 1 - c), "c")
    hidden_part = jnp.where(c == b, half(hidden, c), crossed)
    inner = jnp.stack([half(rows, c), hidden_part])
    inner = lax.all_to_all(jnp.moveaxis(inner, 2, 0), ZA, 0, 0, tiled=True)
    inner = lax.all_gather(inner, DP, axis=0)
    outer_two = lax.all_to_all(jnp.moveaxis(half(grad_two, c), 1, 0), DP, 0, 0, tiled=True)
    outer_one = lax.all_to_all(jnp.moveaxis(half(grad_one, b), 1, 0), DP, 0, 0, tiled=True)
    outer_two = spread(outer_two, FSDP).reshape(4, 2, 2, 4, 2, count, unit)
    outer_one = spread(outer_one, FSDP).reshape(4, 2, 2, 4, 2, count, unit)
    inner = inner.reshape(4, 2, 4, 2, 2, count, unit)
    raw_one = jnp.einsum(
        "yhzark,zahytrm->ktm", inner[:, :, :, :, 0], outer_one, preferred_element_type=jnp.float32
    ).reshape(unit, 2 * unit)
    raw_two = jnp.einsum(
        "yhzark,zatyhrm->ktm", inner[:, :, :, :, 1], outer_two, preferred_element_type=jnp.float32
    ).reshape(unit, 2 * unit)
    squares = jnp.sum(raw_one * raw_one) + jnp.sum(raw_two * raw_two)
    sums = jnp.stack([signed, squares])
    for axes in ("c", "y", "z", ("a", "b")):
        sums = lax.psum(sums, axes)
    width = 16 * unit
    energy_gap = sums[0] / (count * 32 * 80.0 * jnp.sqrt(jnp.float32(width)))
    scale = jnp.sqrt(sums[1] / (2.0 * width * width) + 1e-06)
    return (raw_one / scale, raw_two / scale, energy_gap)


def solution(mesh):
    split = Mesh(mesh.devices.reshape(4, 2, 4, 2, 2), AXES)
    in_specs = (
        P(DP, FSDP), P(DP, FSDP), P(None, DP, FSDP), P(FSDP, None), P(FSDP, None), P(FSDP),
    )
    out_specs = (P(FSDP, DP), P(FSDP, DP), P())
    return jax.shard_map(local, mesh=split, in_specs=in_specs, out_specs=out_specs, check_vma=False)
```

time: 559 us -> 544 us (0.973)
  the two profiles are of different devices: /device:TPU:0 before, /device:TPU:2 now
where the time goes in v1:
time: 544 us; the launch traced here: 533 us
  waiting for transfers between devices  200 us (37%)
  local copies, waits for them, and re-layouts  85.8 us (16%)
  matrix products  78.7 us (14%)
  starting transfers between devices  70.2 us (13%)
  blocking collectives  66.5 us (12%)
  between operations  19.6 us (4%)
  other arithmetic  12.3 us (2%)
    ppermute x25, waiting for transfers between devices, swap(): return lax.ppermute(value, axis, SWAP)  84.7 us
    all_to_all x2, waiting for transfers between devices, spread(): lax.all_to_all(jnp.broadcast_to(value, (count, *value.shape)), axis, 0, 0...  43 us
    dot_general x9, matrix products, back(): lax.dot_general(cotan, flat, (((1,), (1,)), ((), ())), preferred_element_...  40.2 us
    dot_general x10, matrix products, layer(): jnp.einsum('rnk,nkm->nrm', split, block, preferred_element_type=jnp.float32)  32.5 us
    psum x4, blocking collectives, local(): sums = lax.psum(sums, axes)  31.7 us
    ppermute x3, waiting for transfers between devices, gather_second(): moves = (both, *(lax.ppermute(both, 'z', way) for way in (UP, DOWN, OVER)))  25.8 us
    dynamic_update_slice x14, local copies, waits for them, and re-layouts, put(): return lax.dynamic_update_slice(buffer, piece, starts)  22.9 us
    ppermute x25, starting transfers between devices, swap(): return lax.ppermute(value, axis, SWAP)  20.2 us
  transfers between devices with their start and end apart: 46, of which 30 were waited for; matrix products, arithmetic and copies ran while one was open for 20% of the time, Pallas kernels for 0%

profile of v1, /device:TPU:2, one launch (start us, length us, event | category | flops | bytes accessed | tf_op | source)
XLA Modules:
  0.0 532.9 jit_solution(7549971403497703674)
XLA Ops:
  10.9 7.6 %collective-permute-done.12 = bf16[64,8,256]{2,1,0:T(8,128)(2,1)S(1)} collective-permute-done((bf16[64,8,256]{2,1,0:T(8,128)(2,1)S(1)}, bf16[64,8,256]{2,1,0:T(8,128)(2,1)S(1)}, u32[]{:S(2)}, u32[]{:S(2)}) %collective-permute-start.12) | collective-permute-done | bytes 262176 | tf_op jit(solution)/shard_map/ppermute | solution.py:23
  22.8 6.2 %all-to-all-start.1 = ((f32[8,5,16,256]{3,2,1,0:T(8,128)}), f32[8,5,16,256]{3,2,1,0:T(8,128)}, u32[]{:S(2)}, u32[]{:S(2)}) async-start(f32[8,5,16,256]{3,2,1,0:T(8,128)} %copy.129), calls=%async_computation.1 | async-start | bytes 1310720 | tf_op jit(solution)/shard_map/all_to_all | solution.py:83
  57.8 16.4 %collective-permute-done.15 = bf16[2,64,2048]{2,1,0:T(8,128)(2,1)S(1)} collective-permute-done((bf16[2,64,2048]{2,1,0:T(8,128)(2,1)}, bf16[2,64,2048]{2,1,0:T(8,128)(2,1)S(1)}, u32[]{:S(2)}, u32[]{:S(2)}) %collective-permute-start.15) | collective-permute-done | bytes 524320 | tf_op jit(solution)/shard_map/ppermute | solution.py:70
  75.0 9.4 %collective-permute-done.16 = bf16[2,64,2048]{2,1,0:T(8,128)(2,1)S(1)} collective-permute-done((bf16[2,64,2048]{2,1,0:T(8,128)(2,1)}, bf16[2,64,2048]{2,1,0:T(8,128)(2,1)S(1)}, u32[]{:S(2)}, u32[]{:S(2)}) %collective-permute-start.16) | collective-permute-done | bytes 524320 | tf_op jit(solution)/shard_map/ppermute | solution.py:70
  116.4 10.0 %collective-permute-done.8 = bf16[256,2048]{0,1:T(8,128)(2,1)} collective-permute-done((bf16[256,2048]{0,1:T(8,128)(2,1)}, bf16[256,2048]{0,1:T(8,128)(2,1)}, u32[]{:S(2)}, u32[]{:S(2)}) %collective-permute-start.8) | collective-permute-done | bytes 1048608 | tf_op jit(solution)/shard_map/ppermute | solution.py:34
  171.5 14.0 %collective-permute-done.20 = bf16[4,2,32,2048]{3,2,1,0:T(8,128)(2,1)S(1)} collective-permute-done((bf16[4,2,32,2048]{3,2,1,0:T(8,128)(2,1)S(1)}, bf16[4,2,32,2048]{3,2,1,0:T(8,128)(2,1)S(1)}, u32[]{:S(2)}, u32[]{:S(2)}) %collective-permute-start.20) | collective-permute-done | bytes 1048608 | tf_op jit(solution)/shard_map/ppermute | solution.py:36
  191.4 15.9 %all_to_all.41 = f32[8,1,256]{2,1,0:T(1,128)S(1)} all-to-all(f32[8,1,256]{2,1,0:T(1,128)S(1)} %broadcast_in_dim.62), channel_id=1, replica_groups=mesh['y'=4,'c'=2,'z'=4,'a'=2,'b'=2] {'z','a'}, dimensions={0} | all-to-all | bytes 16384 | tf_op jit(solution)/shard_map/all_to_all | solution.py:92
  211.1 6.1 %collective-permute-done.22 = f32[32,2048]{1,0:T(8,128)S(1)} collective-permute-done((f32[32,2048]{1,0:T(8,128)S(1)}, f32[32,2048]{1,0:T(8,128)S(1)}, u32[]{:S(2)}, u32[]{:S(2)}) %collective-permute-start.22) | collective-permute-done | bytes 262176 | tf_op jit(solution)/shard_map/ppermute | solution.py:23
  217.2 6.0 %fusion.41 = f32[32,2048]{1,0:T(8,128)S(1)} fusion(bf16[2048,2048]{1,0:T(8,128)(2,1)} %bitcast.34, f32[32,2048]{1,0:T(8,128)S(1)} %fusion.40, f32[32,2048]{1,0:T(8,128)S(1)} %collective-permute-done.22, f32[32,2048]{1,0:T(8,128)S(1)} %fusion.9, f32[32,2048]{1,0:T(8,128)S(1)} %collective-permute-done.11), kind=kOutput, calls=%fused_computation.111 | convolution fusion | flops 269156352 | bytes 9699328 | tf_op jit(solution)/shard_map/dot_general | solution.py:114
  231.4 7.2 %collective-permute-done.24 = f32[32,2048]{1,0:T(8,128)S(1)} collective-permute-done((f32[32,2048]{1,0:T(8,128)S(1)}, f32[32,2048]{1,0:T(8,128)S(1)}, u32[]{:S(2)}, u32[]{:S(2)}) %collective-permute-start.24) | collective-permute-done | bytes 262176 | tf_op jit(solution)/shard_map/ppermute | solution.py:23
  245.5 7.2 %collective-permute-done.26 = f32[32,2048]{1,0:T(8,128)S(1)} collective-permute-done((f32[32,2048]{1,0:T(8,128)S(1)}, f32[32,2048]{1,0:T(8,128)S(1)}, u32[]{:S(2)}, u32[]{:S(2)}) %collective-permute-start.26) | collective-permute-done | bytes 262176 | tf_op jit(solution)/shard_map/ppermute | solution.py:23
  252.7 6.0 %fusion.43 = f32[32,2048]{1,0:T(8,128)S(1)} fusion(bf16[2048,2048]{1,0:T(8,128)(2,1)} %bitcast.34, f32[32,2048]{1,0:T(8,128)S(1)} %fusion.42, f32[32,2048]{1,0:T(8,128)S(1)} %collective-permute-done.26, f32[32,2048]{1,0:T(8,128)S(1)} %fusion.11, f32[32,2048]{1,0:T(8,128)S(1)} %collective-permute-done.24), kind=kOutput, calls=%fused_computation.113 | convolution fusion | flops 269156352 | bytes 9699328 | tf_op jit(solution)/shard_map/dot_general | solution.py:114
  266.5 7.2 %collective-permute-done.28 = f32[32,2048]{1,0:T(8,128)S(1)} collective-permute-done((f32[32,2048]{1,0:T(8,128)S(1)}, f32[32,2048]{1,0:T(8,128)S(1)}, u32[]{:S(2)}, u32[]{:S(2)}) %collective-permute-start.28) | collective-permute-done | bytes 262176 | tf_op jit(solution)/shard_map/ppermute | solution.py:23
  280.8 7.2 %collective-permute-done.30 = f32[32,2048]{1,0:T(8,128)S(1)} collective-permute-done((f32[32,2048]{1,0:T(8,128)S(1)}, f32[32,2048]{1,0:T(8,128)S(1)}, u32[]{:S(2)}, u32[]{:S(2)}) %collective-permute-start.30) | collective-permute-done | bytes 262176 | tf_op jit(solution)/shard_map/ppermute | solution.py:23
  288.0 6.0 %fusion.45 = f32[32,2048]{1,0:T(8,128)S(1)} fusion(bf16[2048,2048]{1,0:T(8,128)(2,1)} %bitcast.34, f32[32,2048]{1,0:T(8,128)S(1)} %fusion.44, f32[32,2048]{1,0:T(8,128)S(1)} %collective-permute-done.30, f32[32,2048]{1,0:T(8,128)S(1)} %fusion.13, f32[32,2048]{1,0:T(8,128)S(1)} %collective-permute-done.28), kind=kOutput, calls=%fused_computation.115 | convolution fusion | flops 269156352 | bytes 9699328 | tf_op jit(solution)/shard_map/dot_general | solution.py:114
  301.8 7.2 %collective-permute-done.32 = f32[32,2048]{1,0:T(8,128)S(1)} collective-permute-done((f32[32,2048]{1,0:T(8,128)S(1)}, f32[32,2048]{1,0:T(8,128)S(1)}, u32[]{:S(2)}, u32[]{:S(2)}) %collective-permute-start.32) | collective-permute-done | bytes 262176 | tf_op jit(solution)/shard_map/ppermute | solution.py:23
  316.0 10.4 %all_to_all.42 = bf16[8,1,16,256]{3,2,1,0:T(8,128)(2,1)S(1)} all-to-all(bf16[8,1,16,256]{3,2,1,0:T(8,128)(2,1)S(1)} %bitcast.271), channel_id=1, replica_groups=mesh['y'=4,'c'=2,'z'=4,'a'=2,'b'=2] {'z','a'}, dimensions={0} | all-to-all | bytes 131072 | tf_op jit(solution)/shard_map/all_to_all | solution.py:83
  326.6 6.0 %fusion.47 = f32[32,2048]{1,0:T(8,128)S(1)} fusion(bf16[2048,2048]{1,0:T(8,128)(2,1)} %bitcast.34, f32[32,2048]{1,0:T(8,128)S(1)} %fusion.46, f32[32,2048]{1,0:T(8,128)S(1)} %collective-permute-done.34, f32[32,2048]{1,0:T(8,128)S(1)} %fusion.15, f32[32,2048]{1,0:T(8,128)S(1)} %collective-permute-done.32), kind=kOutput, calls=%fused_computation.117 | convolution fusion | flops 269156352 | bytes 9699328 | tf_op jit(solution)/shard_map/dot_general | solution.py:114
  334.3 5.0 convert_reduce_fusion.1
  340.8 12.7 %collective-permute-done.36 = f32[64,2048]{1,0:T(8,128)S(1)} collective-permute-done((f32[64,2048]{1,0:T(8,128)S(1)}, f32[64,2048]{1,0:T(8,128)S(1)}, u32[]{:S(2)}, u32[]{:S(2)}) %collective-permute-start.36) | collective-permute-done | bytes 524320 | tf_op jit(solution)/shard_map/ppermute | solution.py:23
  357.7 6.0 %fusion.99 = f32[64,2048]{1,0:T(8,128)S(1)} fusion(bf16[64,2048]{1,0:T(8,128)(2,1)S(1)} %get-tuple-element.14, bf16[2048,2048]{1,0:T(8,128)(2,1)} %bitcast.224), kind=kOutput, calls=%fused_computation.191 | convolution fusion | flops 536870912 | bytes 9175040 | tf_op jit(solution)/shard_map/dot_general | solution.py:114
  370.3 8.3 %collective-permute-done.39 = f32[64,2048]{1,0:T(8,128)S(1)} collective-permute-done((f32[64,2048]{1,0:T(8,128)S(1)}, f32[64,2048]{1,0:T(8,128)S(1)}, u32[]{:S(2)}, u32[]{:S(2)}) %collective-permute-start.39) | collective-permute-done | bytes 524320 | tf_op jit(solution)/shard_map/ppermute | solution.py:23
  384.4 6.0 %all-to-all-done.6 = bf16[8,32,256]{2,1,0:T(8,128)(2,1)S(1)} async-done(((bf16[8,32,256]{2,1,0:T(8,128)(2,1)}), bf16[8,32,256]{2,1,0:T(8,128)(2,1)S(1)}, u32[]{:S(2)}, u32[]{:S(2)}) %all-to-all-start.6) | async-done | bytes 131104 | tf_op jit(solution)/shard_map/all_to_all | solution.py:156
  390.4 8.5 %all_to_all.43 = bf16[8,32,256]{2,1,0:T(8,128)(2,1)S(1)} all-to-all(bf16[8,32,256]{2,1,0:T(8,128)(2,1)S(1)} %copy.158), channel_id=1, replica_groups=mesh['y'=4,'c'=2,'z'=4,'a'=2,'b'=2] {'y','c'}, dimensions={0} | all-to-all | bytes 262144 | tf_op jit(solution)/shard_map/all_to_all | solution.py:157
  400.5 7.0 %all-to-all-start.7 = ((bf16[16,8,32,256]{3,2,1,0:T(8,128)(2,1)}), bf16[16,8,32,256]{3,2,1,0:T(8,128)(2,1)S(1)}, u32[]{:S(2)}, u32[]{:S(2)}) async-start(bf16[16,8,32,256]{3,2,1,0:T(8,128)(2,1)} %broadcast_in_dim.81), calls=%async_computation.7 | async-start | bytes 4194304 | tf_op jit(solution)/shard_map/all_to_all | solution.py:92
  408.3 26.2 %all-to-all-done.7 = bf16[16,8,32,256]{3,2,1,0:T(8,128)(2,1)S(1)} async-done(((bf16[16,8,32,256]{3,2,1,0:T(8,128)(2,1)}), bf16[16,8,32,256]{3,2,1,0:T(8,128)(2,1)S(1)}, u32[]{:S(2)}, u32[]{:S(2)}) %all-to-all-start.7) | async-done | bytes 2097184 | tf_op jit(solution)/shard_map/all_to_all | solution.py:92
  436.1 8.9 %all-to-all-start.5 = ((bf16[16,8,32,256]{3,2,1,0:T(8,128)(2,1)}), bf16[16,8,32,256]{3,2,1,0:T(8,128)(2,1)}, u32[]{:S(2)}, u32[]{:S(2)}) async-start(bf16[16,8,32,256]{3,2,1,0:T(8,128)(2,1)} %broadcast_in_dim.80), calls=%async_computation.5 | async-start | bytes 4194304 | tf_op jit(solution)/shard_map/all_to_all | solution.py:92
  454.2 16.8 %all-to-all-done.5 = bf16[16,8,32,256]{3,2,1,0:T(8,128)(2,1)} async-done(((bf16[16,8,32,256]{3,2,1,0:T(8,128)(2,1)}), bf16[16,8,32,256]{3,2,1,0:T(8,128)(2,1)}, u32[]{:S(2)}, u32[]{:S(2)}) %all-to-all-start.5) | async-done | bytes 2097184 | tf_op jit(solution)/shard_map/all_to_all | solution.py:92
  471.0 5.3 copy.159
  492.2 8.9 %psum.29 = f32[2]{0:T(128)S(1)} all-reduce(f32[2]{0:T(128)S(1)} %psum.28), channel_id=1, replica_groups=mesh['y'=4,'c'=2,'z'=4,'a'=2,'b'=2] {'y'}, use_global_device_ids=true, to_apply=%region_15.16 | all-reduce | flops 2 | bytes 16 | tf_op jit(solution)/shard_map/psum | solution.py:170
  501.0 9.6 %psum.30 = f32[2]{0:T(128)S(1)} all-reduce(f32[2]{0:T(128)S(1)} %psum.29), channel_id=1, replica_groups=mesh['y'=4,'c'=2,'z'=4,'a'=2,'b'=2] {'z'}, use_global_device_ids=true, to_apply=%region_16.17 | all-reduce | flops 2 | bytes 16 | tf_op jit(solution)/shard_map/psum | solution.py:170
  510.6 10.8 %psum.31 = f32[2]{0:T(128)S(1)} all-reduce(f32[2]{0:T(128)S(1)} %psum.30), channel_id=1, replica_groups=mesh['y'=4,'c'=2,'z'=4,'a'=2,'b'=2] {'a','b'}, use_global_device_ids=true, to_apply=%region_17.18 | all-reduce | flops 2 | bytes 16 | tf_op jit(solution)/shard_map/psum | solution.py:170
  (203 shorter events, 217.7 us)
Async XLA Ops:
  18.6 13.8 %collective-permute-start.13 = (bf16[64,2048]{1,0:T(8,128)(2,1)S(1)}, bf16[64,2048]{1,0:T(8,128)(2,1)S(1)}, u32[]{:S(2)}, u32[]{:S(2)}) collective-permute-start(bf16[64,2048]{1,0:T(8,128)(2,1)S(1)} %bitcast.265), channel_id=1, source_target_pairs={{0,2},{2,0},{1,3},{3,1},{4,6},{6,4},{5,7},{7,5},{8,10},{10,8},{9,1... | collective-permute-start | bytes 786440 | tf_op jit(solution)/shard_map/ppermute | solution.py:23
  22.8 29.4 %all-to-all-start.1 = ((f32[8,5,16,256]{3,2,1,0:T(8,128)}), f32[8,5,16,256]{3,2,1,0:T(8,128)}, u32[]{:S(2)}, u32[]{:S(2)}) async-start(f32[8,5,16,256]{3,2,1,0:T(8,128)} %copy.129), calls=%async_computation.1 | async-start | bytes 1310720 | tf_op jit(solution)/shard_map/all_to_all | solution.py:83
  33.2 20.9 %collective-permute-start.14 = (bf16[2,64,2048]{2,1,0:T(8,128)(2,1)}, bf16[2,64,2048]{2,1,0:T(8,128)(2,1)}, u32[]{:S(2)}, u32[]{:S(2)}) collective-permute-start(bf16[2,64,2048]{2,1,0:T(8,128)(2,1)} %maximum_select_fusion.1), channel_id=1, source_target_pairs={{0,4},{4,8},{8,12},{12,0},{1,5},{5,9},{9,13},{13,1},{2,6},{6,10},{... | collective-permute-start | bytes 1572872 | tf_op jit(solution)/shard_map/ppermute | solution.py:70
  35.3 51.5 %collective-permute-start.2 = (bf16[256,2048]{0,1:T(8,128)(2,1)S(1)}, bf16[256,2048]{0,1:T(8,128)(2,1)S(1)}, u32[]{:S(2)}, u32[]{:S(2)}) collective-permute-start(bf16[256,2048]{0,1:T(8,128)(2,1)S(1)} %bitcast.227), channel_id=1, source_target_pairs={{0,4},{4,8},{8,12},{12,0},{1,5},{5,9},{9,13},{13,1},{2,6},{6,10},{... | collective-permute-start | bytes 3145736 | tf_op jit(solution)/shard_map/ppermute | solution.py:33
  36.9 50.6 %collective-permute-start.3 = (bf16[256,2048]{0,1:T(8,128)(2,1)S(1)}, bf16[256,2048]{0,1:T(8,128)(2,1)}, u32[]{:S(2)}, u32[]{:S(2)}) collective-permute-start(bf16[256,2048]{0,1:T(8,128)(2,1)S(1)} %bitcast.228), channel_id=1, source_target_pairs={{0,12},{4,0},{8,4},{12,8},{1,13},{5,1},{9,5},{13,9},{2,14},{6,2},{... | collective-permute-start | bytes 3145736 | tf_op jit(solution)/shard_map/ppermute | solution.py:34
  38.6 56.4 %collective-permute-start.6 = (bf16[256,2048]{0,1:T(8,128)(2,1)S(1)}, bf16[256,2048]{0,1:T(8,128)(2,1)}, u32[]{:S(2)}, u32[]{:S(2)}) collective-permute-start(bf16[256,2048]{0,1:T(8,128)(2,1)S(1)} %bitcast.229), channel_id=1, source_target_pairs={{0,2},{2,0},{1,3},{3,1},{4,6},{6,4},{5,7},{7,5},{8,10},{10,8},{9,1... | collective-permute-start | bytes 3145736 | tf_op jit(solution)/shard_map/ppermute | solution.py:23
  47.8 26.4 %collective-permute-start.15 = (bf16[2,64,2048]{2,1,0:T(8,128)(2,1)}, bf16[2,64,2048]{2,1,0:T(8,128)(2,1)S(1)}, u32[]{:S(2)}, u32[]{:S(2)}) collective-permute-start(bf16[2,64,2048]{2,1,0:T(8,128)(2,1)} %maximum_select_fusion.1), channel_id=1, source_target_pairs={{0,12},{4,0},{8,4},{12,8},{1,13},{5,1},{9,5},{13,9},{2,14},{6,2},{... | collective-permute-start | bytes 1572872 | tf_op jit(solution)/shard_map/ppermute | solution.py:70
  54.1 30.3 %collective-permute-start.16 = (bf16[2,64,2048]{2,1,0:T(8,128)(2,1)}, bf16[2,64,2048]{2,1,0:T(8,128)(2,1)S(1)}, u32[]{:S(2)}, u32[]{:S(2)}) collective-permute-start(bf16[2,64,2048]{2,1,0:T(8,128)(2,1)} %maximum_select_fusion.1), channel_id=1, source_target_pairs={{0,8},{4,12},{8,0},{12,4},{1,9},{5,13},{9,1},{13,5},{2,10},{6,14},... | collective-permute-start | bytes 1572872 | tf_op jit(solution)/shard_map/ppermute | solution.py:70
  74.2 26.0 %collective-permute-start.1 = (f32[5,16,2048]{2,1,0:T(8,128)}, f32[5,16,2048]{2,1,0:T(8,128)}, u32[]{:S(2)}, u32[]{:S(2)}) collective-permute-start(f32[5,16,2048]{2,1,0:T(8,128)} %bitcast.94), channel_id=1, source_target_pairs={{0,16},{16,0},{1,17},{17,1},{2,18},{18,2},{3,19},{19,3},{4,20},{20... | collective-permute-start | bytes 1966088 | tf_op jit(solution)/shard_map/ppermute | solution.py:23
  85.3 80.8 %collective-permute-start.17 = (bf16[4,2,64,2048]{3,2,1,0:T(8,128)(2,1)}, bf16[4,2,64,2048]{3,2,1,0:T(8,128)(2,1)}, u32[]{:S(2)}, u32[]{:S(2)}) collective-permute-start(bf16[4,2,64,2048]{3,2,1,0:T(8,128)(2,1)} %bitcast_dynamic-update-slice_fusion.3), channel_id=1, source_target_pairs={{0,32},{32,64},{64,96},{96,0},{1,33},{33,65},{65,97},{97,1},{2,34}... | collective-permute-start | bytes 6291464 | tf_op jit(solution)/shard_map/ppermute | solution.py:33
  91.2 15.2 %collective-permute-start.5 = (bf16[128,2048]{0,1:T(8,128)(2,1)}, bf16[128,2048]{0,1:T(8,128)(2,1)}, u32[]{:S(2)}, u32[]{:S(2)}) collective-permute-start(bf16[128,2048]{0,1:T(8,128)(2,1)} %slice.68), channel_id=1, source_target_pairs={{0,12},{4,0},{8,4},{12,8},{1,13},{5,1},{9,5},{13,9},{2,14},{6,2},{... | collective-permute-start | bytes 1572872 | tf_op jit(solution)/shard_map/ppermute | solution.py:36
  95.0 16.4 %collective-permute-start.4 = (bf16[128,2048]{0,1:T(8,128)(2,1)}, bf16[128,2048]{0,1:T(8,128)(2,1)}, u32[]{:S(2)}, u32[]{:S(2)}) collective-permute-start(bf16[128,2048]{0,1:T(8,128)(2,1)} %slice.67), channel_id=1, source_target_pairs={{0,4},{4,8},{8,12},{12,0},{1,5},{5,9},{9,13},{13,1},{2,6},{6,10},{... | collective-permute-start | bytes 1572872 | tf_op jit(solution)/shard_map/ppermute | solution.py:35
  97.3 33.5 %collective-permute-start.7 = (bf16[256,2048]{0,1:T(8,128)(2,1)}, bf16[256,2048]{0,1:T(8,128)(2,1)}, u32[]{:S(2)}, u32[]{:S(2)}) collective-permute-start(bf16[256,2048]{0,1:T(8,128)(2,1)} %collective-permute-done.6), channel_id=1, source_target_pairs={{0,4},{4,8},{8,12},{12,0},{1,5},{5,9},{9,13},{13,1},{2,6},{6,10},{... | collective-permute-start | bytes 3145736 | tf_op jit(solution)/shard_map/ppermute | solution.py:33
  100.2 26.3 %collective-permute-start.8 = (bf16[256,2048]{0,1:T(8,128)(2,1)}, bf16[256,2048]{0,1:T(8,128)(2,1)}, u32[]{:S(2)}, u32[]{:S(2)}) collective-permute-start(bf16[256,2048]{0,1:T(8,128)(2,1)} %collective-permute-done.6), channel_id=1, source_target_pairs={{0,12},{4,0},{8,4},{12,8},{1,13},{5,1},{9,5},{13,9},{2,14},{6,2},{... | collective-permute-start | bytes 3145736 | tf_op jit(solution)/shard_map/ppermute | solution.py:34
  106.4 56.6 %collective-permute-start.18 = (bf16[4,2,64,2048]{3,2,1,0:T(8,128)(2,1)}, bf16[4,2,64,2048]{3,2,1,0:T(8,128)(2,1)}, u32[]{:S(2)}, u32[]{:S(2)}) collective-permute-start(bf16[4,2,64,2048]{3,2,1,0:T(8,128)(2,1)} %bitcast_dynamic-update-slice_fusion.3), channel_id=1, source_target_pairs={{0,96},{32,0},{64,32},{96,64},{1,97},{33,1},{65,33},{97,65},{2,98}... | collective-permute-start | bytes 6291464 | tf_op jit(solution)/shard_map/ppermute | solution.py:34
  128.3 14.1 %collective-permute-start.10 = (bf16[128,2048]{0,1:T(8,128)(2,1)}, bf16[128,2048]{0,1:T(8,128)(2,1)}, u32[]{:S(2)}, u32[]{:S(2)}) collective-permute-start(bf16[128,2048]{0,1:T(8,128)(2,1)} %slice.70), channel_id=1, source_target_pairs={{0,12},{4,0},{8,4},{12,8},{1,13},{5,1},{9,5},{13,9},{2,14},{6,2},{... | collective-permute-start | bytes 1572872 | tf_op jit(solution)/shard_map/ppermute | solution.py:36
  132.7 13.7 %collective-permute-start.9 = (bf16[128,2048]{0,1:T(8,128)(2,1)}, bf16[128,2048]{0,1:T(8,128)(2,1)}, u32[]{:S(2)}, u32[]{:S(2)}) collective-permute-start(bf16[128,2048]{0,1:T(8,128)(2,1)} %slice.69), channel_id=1, source_target_pairs={{0,4},{4,8},{8,12},{12,0},{1,5},{5,9},{9,13},{13,1},{2,6},{6,10},{... | collective-permute-start | bytes 1572872 | tf_op jit(solution)/shard_map/ppermute | solution.py:35
  164.3 21.2 %collective-permute-start.20 = (bf16[4,2,32,2048]{3,2,1,0:T(8,128)(2,1)S(1)}, bf16[4,2,32,2048]{3,2,1,0:T(8,128)(2,1)S(1)}, u32[]{:S(2)}, u32[]{:S(2)}) collective-permute-start(bf16[4,2,32,2048]{3,2,1,0:T(8,128)(2,1)S(1)} %slice.72), channel_id=1, source_target_pairs={{0,96},{32,0},{64,32},{96,64},{1,97},{33,1},{65,33},{97,65},{2,98}... | collective-permute-start | bytes 3145736 | tf_op jit(solution)/shard_map/ppermute | solution.py:36
  167.4 22.1 %collective-permute-start.19 = (bf16[4,2,32,2048]{3,2,1,0:T(8,128)(2,1)S(1)}, bf16[4,2,32,2048]{3,2,1,0:T(8,128)(2,1)S(1)}, u32[]{:S(2)}, u32[]{:S(2)}) collective-permute-start(bf16[4,2,32,2048]{3,2,1,0:T(8,128)(2,1)S(1)} %slice.71), channel_id=1, source_target_pairs={{0,32},{32,64},{64,96},{96,0},{1,33},{33,65},{65,97},{97,1},{2,34}... | collective-permute-start | bytes 3145736 | tf_op jit(solution)/shard_map/ppermute | solution.py:35
  191.3 16.0 %collective-permute-start.21 = (f32[32,2048]{1,0:T(8,128)S(1)}, f32[32,2048]{1,0:T(8,128)S(1)}, u32[]{:S(2)}, u32[]{:S(2)}) collective-permute-start(f32[32,2048]{1,0:T(8,128)S(1)} %fusion.10), channel_id=1, source_target_pairs={{0,16},{16,0},{1,17},{17,1},{2,18},{18,2},{3,19},{19,3},{4,20},{20... | collective-permute-start | bytes 786440 | tf_op jit(solution)/shard_map/ppermute | solution.py:23
  230.1 8.4 %collective-permute-start.24 = (f32[32,2048]{1,0:T(8,128)S(1)}, f32[32,2048]{1,0:T(8,128)S(1)}, u32[]{:S(2)}, u32[]{:S(2)}) collective-permute-start(f32[32,2048]{1,0:T(8,128)S(1)} %fusion.11), channel_id=1, source_target_pairs={{0,1},{1,0},{2,3},{3,2},{4,5},{5,4},{6,7},{7,6},{8,9},{9,8},{10,11... | collective-permute-start | bytes 786440 | tf_op jit(solution)/shard_map/ppermute | solution.py:23
  265.2 8.4 %collective-permute-start.28 = (f32[32,2048]{1,0:T(8,128)S(1)}, f32[32,2048]{1,0:T(8,128)S(1)}, u32[]{:S(2)}, u32[]{:S(2)}) collective-permute-start(f32[32,2048]{1,0:T(8,128)S(1)} %fusion.13), channel_id=1, source_target_pairs={{0,1},{1,0},{2,3},{3,2},{4,5},{5,4},{6,7},{7,6},{8,9},{9,8},{10,11... | collective-permute-start | bytes 786440 | tf_op jit(solution)/shard_map/ppermute | solution.py:23
  300.5 8.4 %collective-permute-start.32 = (f32[32,2048]{1,0:T(8,128)S(1)}, f32[32,2048]{1,0:T(8,128)S(1)}, u32[]{:S(2)}, u32[]{:S(2)}) collective-permute-start(f32[32,2048]{1,0:T(8,128)S(1)} %fusion.15), channel_id=1, source_target_pairs={{0,1},{1,0},{2,3},{3,2},{4,5},{5,4},{6,7},{7,6},{8,9},{9,8},{10,11... | collective-permute-start | bytes 786440 | tf_op jit(solution)/shard_map/ppermute | solution.py:23
  314.8 11.8 %collective-permute-start.34 = (f32[32,2048]{1,0:T(8,128)S(1)}, f32[32,2048]{1,0:T(8,128)S(1)}, u32[]{:S(2)}, u32[]{:S(2)}) collective-permute-start(f32[32,2048]{1,0:T(8,128)S(1)} %fusion.46), channel_id=1, source_target_pairs={{0,1},{1,0},{2,3},{3,2},{4,5},{5,4},{6,7},{7,6},{8,9},{9,8},{10,11... | collective-permute-start | bytes 786440 | tf_op jit(solution)/shard_map/ppermute | solution.py:23
  339.3 14.3 %collective-permute-start.36 = (f32[64,2048]{1,0:T(8,128)S(1)}, f32[64,2048]{1,0:T(8,128)S(1)}, u32[]{:S(2)}, u32[]{:S(2)}) collective-permute-start(f32[64,2048]{1,0:T(8,128)S(1)} %convert_reduce_fusion.1), channel_id=1, source_target_pairs={{0,1},{1,0},{2,3},{3,2},{4,5},{5,4},{6,7},{7,6},{8,9},{9,8},{10,11... | collective-permute-start | bytes 1572872 | tf_op jit(solution)/shard_map/ppermute | solution.py:23
  355.7 9.6 %collective-permute-start.37 = (bf16[32,8,256]{2,0,1:T(8,128)(2,1)S(1)}, bf16[32,8,256]{2,0,1:T(8,128)(2,1)S(1)}, u32[]{:S(2)}, u32[]{:S(2)}) collective-permute-start(bf16[32,8,256]{2,0,1:T(8,128)(2,1)S(1)} %bitcast.270), channel_id=1, source_target_pairs={{0,16},{16,0},{1,17},{17,1},{2,18},{18,2},{3,19},{19,3},{4,20},{20... | collective-permute-start | bytes 393224 | tf_op jit(solution)/shard_map/ppermute | solution.py:23
  363.7 14.8 %collective-permute-start.39 = (f32[64,2048]{1,0:T(8,128)S(1)}, f32[64,2048]{1,0:T(8,128)S(1)}, u32[]{:S(2)}, u32[]{:S(2)}) collective-permute-start(f32[64,2048]{1,0:T(8,128)S(1)} %fusion.99), channel_id=1, source_target_pairs={{0,1},{1,0},{2,3},{3,2},{4,5},{5,4},{6,7},{7,6},{8,9},{9,8},{10,11... | collective-permute-start | bytes 1572872 | tf_op jit(solution)/shard_map/ppermute | solution.py:23
  366.1 14.9 %all-to-all-start.3 = ((bf16[8,2,32,256]{3,2,1,0:T(8,128)(2,1)}), bf16[8,2,32,256]{3,2,1,0:T(8,128)(2,1)S(1)}, u32[]{:S(2)}, u32[]{:S(2)}) async-start(bf16[8,2,32,256]{3,2,1,0:T(8,128)(2,1)} %maximum_bitcast_fusion.4), calls=%async_computation.3 | async-start | bytes 524288 | tf_op jit(solution)/shard_map/all_to_all | solution.py:154
  381.0 9.4 %all-to-all-start.6 = ((bf16[8,32,256]{2,1,0:T(8,128)(2,1)}), bf16[8,32,256]{2,1,0:T(8,128)(2,1)S(1)}, u32[]{:S(2)}, u32[]{:S(2)}) async-start(bf16[8,32,256]{2,1,0:T(8,128)(2,1)} %copy.161), calls=%async_computation.6 | async-start | bytes 262144 | tf_op jit(solution)/shard_map/all_to_all | solution.py:156
  400.5 34.0 %all-to-all-start.7 = ((bf16[16,8,32,256]{3,2,1,0:T(8,128)(2,1)}), bf16[16,8,32,256]{3,2,1,0:T(8,128)(2,1)S(1)}, u32[]{:S(2)}, u32[]{:S(2)}) async-start(bf16[16,8,32,256]{3,2,1,0:T(8,128)(2,1)} %broadcast_in_dim.81), calls=%async_computation.7 | async-start | bytes 4194304 | tf_op jit(solution)/shard_map/all_to_all | solution.py:92
  407.5 73.1 %all-gather.3.cloned.1.call-start = ((), (), s32[]{:S(2)}) async-start(), calls=%async_computation.8 | async-start | bytes 2359296 | tf_op jit(solution)/shard_map/all_gather | solution.py:155
  436.1 34.9 %all-to-all-start.5 = ((bf16[16,8,32,256]{3,2,1,0:T(8,128)(2,1)}), bf16[16,8,32,256]{3,2,1,0:T(8,128)(2,1)}, u32[]{:S(2)}, u32[]{:S(2)}) async-start(bf16[16,8,32,256]{3,2,1,0:T(8,128)(2,1)} %broadcast_in_dim.80), calls=%async_computation.5 | async-start | bytes 4194304 | tf_op jit(solution)/shard_map/all_to_all | solution.py:92
  (23 other events, 353.3 us)
Sparse Core Ops, SparseCore 0:
  410.7 24.3 all-gather.2

commit v2 on v1

v2 whole, which is shorter than its diff:
```python
import jax
import jax.numpy as jnp
from jax import lax
from jax.experimental import pallas as pl
from jax.experimental.pallas import tpu as pltpu
from jax.sharding import Mesh
from jax.sharding import PartitionSpec as P

STEPS = 4
AXES = ("y", "c", "z", "a", "b")
DP = ("y", "c")
ZA = ("z", "a")
FSDP = ("z", "a", "b")
X = ("a", "b")


def pick(value, index, dim):
    return lax.dynamic_index_in_dim(value, index, dim, keepdims=False)


def send(value, axis, step):
    count = lax.axis_size(axis)
    return lax.ppermute(value, axis, [(j, j ^ step) for j in range(count)])


def swap(value, axis):
    return send(value, axis, 1)


def from_all(value, axis):
    near = {step: send(value, axis, step) for step in (1, 3, 2)}
    return [value, near[1], near[2], near[3]]


def to_each(values, axis):
    near = {step: send(values[step], axis, step) for step in (1, 3, 2)}
    return [values[0], near[1], near[2], near[3]]


def total(value, axis):
    parts = from_all(value, axis)
    return (parts[0] + parts[1]) + (parts[2] + parts[3])


def relative(value, axis, dim):
    me = lax.axis_index(axis)
    return jnp.stack([pick(value, me ^ k, dim) for k in range(value.shape[dim])], axis=dim)


def put(buffer, piece, starts):
    starts = tuple(starts) + (0,) * (buffer.ndim - len(starts))
    return lax.dynamic_update_slice(buffer, piece, starts)


def both_ways(left, right, axis):
    left_one, right_three = send(left, axis, 1), send(right, axis, 3)
    left_three, right_one = send(left, axis, 3), send(right, axis, 1)
    left_two = send(left_one, axis, 3)
    right_two = send(right_three, axis, 1)
    return ([left, left_one, left_two, left_three], [right, right_one, right_two, right_three])


def gather_second_column(weight, c, b):
    rows, cols = weight.shape
    unit = cols // 16
    part = rows // 4
    y = lax.axis_index("y")
    mine = lax.dynamic_slice_in_dim(weight, y * part, part, 0).reshape(part, 8, 2, unit)
    theirs = swap(pick(mine, 1 - b, 2).reshape(part, 8 * unit), "b")
    piece = jnp.where(c == b, pick(mine, b, 2).reshape(part, 8 * unit), theirs)
    across = swap(piece, "a")
    return both_ways(piece, across, "z")


def gather_second(column):
    part, width = column[0][0].shape
    me = {axis: lax.axis_index(axis) for axis in ("y", "z", "a")}
    stacks = [jnp.concatenate(pieces, axis=0) for pieces in column]
    moved = both_ways(*stacks, "y")
    out = jnp.zeros((4, 2, 4, part, width), column[0][0].dtype)
    for ky in (0, 1, 3, 2):
        for ka in (0, 1):
            pieces = moved[ka][ky].reshape(4, 1, 1, part, width)
            for kz in range(4):
                out = put(
                    out, pieces[kz : kz + 1], (me["z"] ^ kz, me["a"] ^ ka, me["y"] ^ ky)
                )
    return out.reshape(8, 4 * part, width)


def first_piece(weight, c):
    rows, cols = weight.shape
    unit = cols // 16
    piece = pick(weight.reshape(rows, 8, 2, unit), c, 2).reshape(rows, 8 * unit)
    return (piece, swap(piece, "a"))


def gather_first(piece, across):
    own, other = both_ways(piece, across, "z")
    return jnp.stack([part for pair in zip(own, other) for part in pair])


def to_groups(value):
    lead, rows, cols = value.shape
    part = rows // 8
    split = jnp.moveaxis(value.reshape(lead, 8, part, cols), 1, 0)
    got = lax.all_to_all(split, ZA, 0, 0, tiled=True).reshape(4, 2, lead, part, cols)
    got = relative(relative(got, "z", 0), "a", 1).reshape(8, lead, part, cols)
    own = jnp.transpose(got, (1, 2, 0, 3)).reshape(lead, part, 8 * cols)
    return by_index("c", own, swap(own, "c"), 1)


def by_index(axis, own, other, dim):
    first = lax.axis_index(axis) == 0
    return jnp.concatenate(
        [jnp.where(first, own, other), jnp.where(first, other, own)], axis=dim
    )


def spread(value, axis):
    count = lax.axis_size(axis)
    return lax.all_to_all(jnp.broadcast_to(value, (count, *value.shape)), axis, 0, 0, tiled=True)


def slope(values):
    sig = jax.nn.sigmoid(values)
    return sig * (1.0 + values * (1.0 - sig))


def share(part, axis, narrow):
    if narrow and axis == "b":
        part = part.astype(jnp.bfloat16)
    return part.astype(jnp.float32) + swap(part, axis).astype(jnp.float32)


def layer(inputs, block, axis, narrow):
    slices, depth, _ = block.shape
    split = inputs.reshape(inputs.shape[0], slices, depth)
    terms = jnp.einsum("rnk,nkm->nrm", split, block, preferred_element_type=jnp.float32)
    part = jnp.sum(terms.astype(jnp.bfloat16).astype(jnp.float32), axis=0)
    return share(part, axis, narrow)


def back(cotan, block, axis, narrow):
    flat = block.reshape(-1, block.shape[-1])
    part = lax.dot_general(
        cotan, flat, (((1,), (1,)), ((), ())), preferred_element_type=jnp.float32
    )
    return share(part, axis, narrow)


def one_pass(inputs, cotan, readout, first, second, narrow):
    pre_one = layer(inputs, first, "b", narrow)
    hidden = jax.nn.silu(pre_one).astype(jnp.bfloat16)
    pre_two = layer(hidden, second, "c", narrow)
    grad_two = (cotan[:, None] * readout[None, :] * slope(pre_two)).astype(jnp.bfloat16)
    grad_one = (back(grad_two, second, "b", narrow) * slope(pre_one)).astype(jnp.bfloat16)
    return (hidden, pre_two, grad_two, grad_one)


def products(u_ref, g_ref, h_ref, q_ref, one_ref, two_ref, sum_ref):
    one = jnp.dot(u_ref[...], g_ref[...], preferred_element_type=jnp.float32)
    one_ref[...] = one
    two = jnp.dot(h_ref[...], q_ref[...], preferred_element_type=jnp.float32)
    two_ref[...] = two
    sum_ref[...] = jnp.full(sum_ref.shape, jnp.sum(one * one) + jnp.sum(two * two))


def contract(u, g, h, q):
    tile = jax.ShapeDtypeStruct((u.shape[0], g.shape[1]), jnp.float32)
    return pl.pallas_call(
        products,
        out_shape=(tile, tile, jax.ShapeDtypeStruct((8, 128), jnp.float32)),
        compiler_params=pltpu.CompilerParams(vmem_limit_bytes=32 * 1024 * 1024),
    )(u, g, h, q)


def rows_to_owner(rows, hidden, c, b):
    count = rows.shape[0] // 2
    unit = rows.shape[1] // 8
    half = lambda value, at: pick(value.reshape(2, count, 4, 2, unit), at, 0)
    crossed = swap(half(hidden, 1 - c), "c")
    hidden_part = jnp.where(c == b, half(hidden, c), crossed)
    hidden_part = relative(relative(hidden_part, "z", 1), "a", 2)
    parts = jnp.concatenate([half(rows, c), hidden_part], axis=-1)
    parts = jnp.transpose(parts, (2, 1, 0, 3))
    pairs = jnp.stack([parts[0], swap(parts[1], "a")], axis=1)
    column = jnp.stack(to_each([pairs[k] for k in range(4)], "z"))
    plane = jnp.stack(from_all(column, "y"))
    return by_index("c", plane[None], swap(plane, "c")[None], 0)


def second_to_owner(grad, c):
    count = grad.shape[0] // 2
    unit = grad.shape[1] // 8
    mine = pick(grad.reshape(2, count, 4, 2, unit), c, 0)
    parts = jnp.transpose(relative(relative(mine, "y", 1), "c", 2), (2, 1, 0, 3))
    pairs = by_index("c", parts[0][:, None], swap(parts[1], "c")[:, None], 1)
    block = jnp.stack(to_each([pairs[k] for k in range(4)], "y"))
    near = from_all(block, X)
    row = jnp.stack([by_index("b", near[2 * k], near[2 * k + 1], -1) for k in range(2)])
    return jnp.stack(from_all(row, "z")).reshape(-1, 2 * unit)


def first_to_owner(grad, b):
    count = grad.shape[0] // 2
    unit = grad.shape[1] // 8
    mine = pick(grad.reshape(2, count, 4, 2, unit), b, 0)
    parts = jnp.transpose(relative(relative(mine, "y", 1), "c", 2), (2, 1, 0, 3))
    pairs = by_index("c", parts[0], swap(parts[1], "c"), -1)
    block = jnp.stack(to_each([pairs[k] for k in range(4)], "y"))
    column = jnp.stack(from_all(block, "z"))
    near = from_all(column, X)
    return jnp.stack(
        [by_index("b", near[2 * k][None], near[2 * k + 1][None], 0) for k in range(2)]
    ).reshape(-1, 2 * unit)


def local(data_samples, negative_start, langevin_noise, first_weight, second_weight, readout):
    c, b = lax.axis_index("c"), lax.axis_index("b")
    column = gather_second_column(second_weight, c, b)
    piece, across = first_piece(first_weight, c)
    tied = lax.optimization_barrier((piece, across, column[0][1], column[1][3]))
    piece, across = tied[:2]
    column[0][1], column[1][3] = tied[2:]
    first = gather_first(piece, across)
    start = jnp.concatenate([negative_start[None], langevin_noise])
    start, data, readout, column = lax.optimization_barrier(
        (start, data_samples[None], readout, column)
    )
    second = gather_second(column)
    moved_in = to_groups(start)
    data = to_groups(data)[0]
    state, noise = (moved_in[0], moved_in[1:])
    readout = spread(readout, ZA).reshape(-1)
    count = state.shape[0]
    ones = jnp.ones((count,), jnp.float32)
    for step in range(STEPS):
        inputs = state.astype(jnp.bfloat16)
        grad_one = one_pass(inputs, ones, readout, first, second, True)[3]
        state = state - 0.005 * back(grad_one, first, "c", True) + 0.1 * noise[step]
    rows = jnp.concatenate([data, state.astype(jnp.bfloat16)], axis=0)
    cotan = jnp.concatenate([ones, -ones])
    hidden, pre_two, grad_two, grad_one = one_pass(rows, cotan, readout, first, second, False)
    energies = jnp.sum(jax.nn.silu(pre_two) * readout[None, :], axis=1)
    signed = 0.5 * jnp.sum(cotan * energies)

    unit = rows.shape[1] // 8
    inner = rows_to_owner(rows, hidden, c, b)
    u = jnp.transpose(inner[..., :unit], (5, 3, 0, 2, 1, 4)).reshape(unit, -1)
    h = jnp.transpose(inner[..., unit:], (5, 2, 3, 1, 0, 4)).reshape(unit, -1)
    g = first_to_owner(grad_one, b)
    q = second_to_owner(grad_two, c)
    raw_one, raw_two, squares = contract(u, g, h, q)
    sums = jnp.where(lax.broadcasted_iota(jnp.int32, squares.shape, 0) == 0, squares, signed)
    sums = sums + swap(sums, "c")
    for axis in ("y", "z", X):
        sums = total(sums, axis)
    width = 16 * unit
    energy_gap = sums[1, 0] / (count * 32 * 80.0 * jnp.sqrt(jnp.float32(width)))
    scale = jnp.sqrt(sums[0, 0] / (2.0 * width * width) + 1e-06)
    return (raw_one / scale, raw_two / scale, energy_gap)


def solution(mesh):
    split = Mesh(mesh.devices.reshape(4, 2, 4, 2, 2), AXES)
    in_specs = (
        P(DP, FSDP), P(DP, FSDP), P(None, DP, FSDP), P(FSDP, None), P(FSDP, None), P(FSDP),
    )
    out_specs = (P(FSDP, DP), P(FSDP, DP), P())
    return jax.shard_map(local, mesh=split, in_specs=in_specs, out_specs=out_specs, check_vma=False)
```

time: 544 us -> 535 us (0.983)
  the two profiles are of different devices: /device:TPU:2 before, /device:TPU:0 now
where the time goes in v2:
time: 535 us; the launch traced here: 525 us
  waiting for transfers between devices  206 us (39%)
  matrix products  103 us (19%)
  starting transfers between devices  102 us (19%)
  local copies, waits for them, and re-layouts  76.4 us (14%)
  other arithmetic  16.5 us (3%)
  blocking collectives  13.3 us (2%)
  between operations  5.36 us (1%)
    ppermute x81, waiting for transfers between devices, send(): return lax.ppermute(value, axis, [(j, j ^ step) for j in range(count)])  184 us
    ppermute x81, starting transfers between devices, send(): return lax.ppermute(value, axis, [(j, j ^ step) for j in range(count)])  92.4 us
    dot_general x9, matrix products, back(): lax.dot_general(cotan, flat, (((1,), (1,)), ((), ())), preferred_element_...  53.7 us
    dot_general x10, matrix products, layer(): jnp.einsum('rnk,nkm->nrm', split, block, preferred_element_type=jnp.float32)  49.5 us
    dynamic_update_slice x32, local copies, waits for them, and re-layouts, put(): return lax.dynamic_update_slice(buffer, piece, starts)  29 us
    all_to_all x2, waiting for transfers between devices, to_groups(): lax.all_to_all(split, ZA, 0, 0, tiled=True).reshape(4, 2, lead, part, cols)  22.3 us
    unnamed x56, local copies, waits for them, and re-layouts  21.2 us
    all_to_all x1, blocking collectives, spread(): lax.all_to_all(jnp.broadcast_to(value, (count, *value.shape)), axis, 0, 0...  13.3 us
  transfers between devices with their start and end apart: 83, of which 44 were waited for; matrix products, arithmetic and copies ran while one was open for 20% of the time, Pallas kernels for 0%

profile of v2, /device:TPU:0, one launch (start us, length us, event | category | flops | bytes accessed | tf_op | source)
XLA Modules:
  0.0 524.8 jit_solution(2535209999343653576)
XLA Ops:
  10.8 6.2 %dynamic-slice_reduce_fusion = bf16[256,8,256]{2,1,0:T(8,128)(2,1)S(1)} fusion(bf16[256,8,2,256]{3,2,1,0:T(2,128)(2,1)S(1)} %reshape.192, s32[]{:T(128)S(6)} %select_n.337), kind=kLoop, calls=%fused_computation.24 | loop fusion | bytes 2097156 | tf_op jit(solution)/shard_map/jit(dynamic_index_in_dim)/dynamic_slice | solution.py:18
  23.1 25.9 %collective-permute-done.3 = bf16[64,2048]{1,0:T(8,128)(2,1)S(1)} collective-permute-done((bf16[64,2048]{1,0:T(8,128)(2,1)S(1)}, bf16[64,2048]{1,0:T(8,128)(2,1)S(1)}, u32[]{:S(2)}, u32[]{:S(2)}) %collective-permute-start.3) | collective-permute-done | bytes 262176 | tf_op jit(solution)/shard_map/ppermute | solution.py:23
  73.7 6.4 %all-to-all-start.1 = ((f32[8,5,16,256]{3,2,1,0:T(8,128)}), f32[8,5,16,256]{3,2,1,0:T(8,128)S(1)}, u32[]{:S(2)}, u32[]{:S(2)}) async-start(f32[8,5,16,256]{3,2,1,0:T(8,128)} %copy.162), calls=%async_computation.1 | async-start | bytes 1310720 | tf_op jit(solution)/shard_map/all_to_all | solution.py:107
  102.1 21.5 %all-to-all-done.1 = f32[8,5,16,256]{3,2,1,0:T(8,128)S(1)} async-done(((f32[8,5,16,256]{3,2,1,0:T(8,128)}), f32[8,5,16,256]{3,2,1,0:T(8,128)S(1)}, u32[]{:S(2)}, u32[]{:S(2)}) %all-to-all-start.1) | async-done | bytes 655392 | tf_op jit(solution)/shard_map/all_to_all | solution.py:107
  132.6 14.2 %collective-permute-done.19 = bf16[256,2048]{1,0:T(8,128)(2,1)S(1)} collective-permute-done((bf16[256,2048]{1,0:T(8,128)(2,1)}, bf16[256,2048]{1,0:T(8,128)(2,1)S(1)}, u32[]{:S(2)}, u32[]{:S(2)}) %collective-permute-start.19) | collective-permute-done | bytes 1048608 | tf_op jit(solution)/shard_map/ppermute | solution.py:23
  152.8 17.4 %collective-permute-done.20 = bf16[256,2048]{1,0:T(8,128)(2,1)S(1)} collective-permute-done((bf16[256,2048]{1,0:T(8,128)(2,1)}, bf16[256,2048]{1,0:T(8,128)(2,1)S(1)}, u32[]{:S(2)}, u32[]{:S(2)}) %collective-permute-start.20) | collective-permute-done | bytes 1048608 | tf_op jit(solution)/shard_map/ppermute | solution.py:23
  183.1 10.3 %collective-permute-done.21 = bf16[256,2048]{1,0:T(8,128)(2,1)S(1)} collective-permute-done((bf16[256,2048]{1,0:T(8,128)(2,1)}, bf16[256,2048]{1,0:T(8,128)(2,1)S(1)}, u32[]{:S(2)}, u32[]{:S(2)}) %collective-permute-start.21) | collective-permute-done | bytes 1048608 | tf_op jit(solution)/shard_map/ppermute | solution.py:23
  199.7 5.7 %collective-permute-done.13 = bf16[256,2048]{1,0:T(8,128)(2,1)S(1)} collective-permute-done((bf16[256,2048]{1,0:T(8,128)(2,1)}, bf16[256,2048]{1,0:T(8,128)(2,1)S(1)}, u32[]{:S(2)}, u32[]{:S(2)}) %collective-permute-start.13) | collective-permute-done | bytes 1048608 | tf_op jit(solution)/shard_map/ppermute | solution.py:23
  206.4 11.1 %collective-permute-done.15 = bf16[256,2048]{1,0:T(8,128)(2,1)S(1)} collective-permute-done((bf16[256,2048]{1,0:T(8,128)(2,1)}, bf16[256,2048]{1,0:T(8,128)(2,1)S(1)}, u32[]{:S(2)}, u32[]{:S(2)}) %collective-permute-start.15) | collective-permute-done | bytes 1048608 | tf_op jit(solution)/shard_map/ppermute | solution.py:23
  234.8 4.9 fusion.4
  239.9 13.3 %all_to_all.16 = f32[8,1,256]{2,1,0:T(1,128)S(1)} all-to-all(f32[8,1,256]{2,1,0:T(1,128)S(1)} %broadcast_in_dim.25), channel_id=1, replica_groups=mesh['y'=4,'c'=2,'z'=4,'a'=2,'b'=2] {'z','a'}, dimensions={0} | all-to-all | bytes 16384 | tf_op jit(solution)/shard_map/all_to_all | solution.py:122
  253.1 6.0 %convolution_convert_fusion.13 = bf16[32,2048]{1,0:T(8,128)(2,1)S(1)} fusion(bf16[2048,2048]{1,0:T(8,128)(2,1)} %bitcast.55, f32[32,2048]{1,0:T(8,128)S(1)} %fusion.4, f32[32,2048]{1,0:T(8,128)S(1)} %collective-permute-done.24, f32[2048]{0:T(1024)S(1)} %bitcast.435), kind=kOutput, calls=%fused_computation.19 | convolution fusion | flops 269156352 | bytes 9052160 | tf_op jit(solution)/shard_map/dot_general | solution.py:146
  264.1 6.0 %fusion.61 = f32[32,2048]{1,0:T(8,128)S(1)} fusion(bf16[2048,2048]{1,0:T(8,128)(2,1)} %bitcast.56, bf16[32,2048]{1,0:T(8,128)(2,1)S(1)} %collective-permute-done.25, bf16[32,2048]{1,0:T(8,128)(2,1)S(1)} %convolution_convert_fusion.13, bf16[32,2048]{1,0:T(8,128)(2,1)S(1)} %collective-permute-done.17, bf16[32,2048]{1,0:T(8,128)(2,1)S(1)} %fusion.8), kind=kOutput, calls=%fused_computation.204 | convolution fusion | flops 269418496 | bytes 9175040 | tf_op jit(solution)/shard_map/dot_general | solution.py:146
  277.3 4.9 collective-permute-done.27
  282.3 4.9 fusion.5
  288.9 6.0 %convolution_convert_fusion.12 = bf16[32,2048]{1,0:T(8,128)(2,1)S(1)} fusion(bf16[2048,2048]{1,0:T(8,128)(2,1)} %bitcast.55, f32[32,2048]{1,0:T(8,128)S(1)} %fusion.5, f32[32,2048]{1,0:T(8,128)S(1)} %collective-permute-done.28, f32[2048]{0:T(1024)S(1)} %bitcast.436), kind=kOutput, calls=%fused_computation.18 | convolution fusion | flops 269156352 | bytes 9052160 | tf_op jit(solution)/shard_map/dot_general | solution.py:146
  295.5 4.9 collective-permute-done.29
  300.4 6.0 %fusion.62 = f32[32,2048]{1,0:T(8,128)S(1)} fusion(bf16[2048,2048]{1,0:T(8,128)(2,1)} %bitcast.56, bf16[32,2048]{1,0:T(8,128)(2,1)S(1)} %collective-permute-done.29, bf16[32,2048]{1,0:T(8,128)(2,1)S(1)} %convolution_convert_fusion.12, bf16[32,2048]{1,0:T(8,128)(2,1)S(1)} %collective-permute-done.27, bf16[32,2048]{1,0:T(8,128)(2,1)S(1)} %fusion.9), kind=kOutput, calls=%fused_computation.205 | convolution fusion | flops 269418496 | bytes 9175040 | tf_op jit(solution)/shard_map/dot_general | solution.py:146
  308.4 4.9 fusion.10
  314.0 5.0 collective-permute-done.31
  319.1 4.9 fusion.6
  325.6 5.9 %convolution_convert_fusion.11 = bf16[32,2048]{1,0:T(8,128)(2,1)S(1)} fusion(bf16[2048,2048]{1,0:T(8,128)(2,1)} %bitcast.55, f32[32,2048]{1,0:T(8,128)S(1)} %fusion.6, f32[32,2048]{1,0:T(8,128)S(1)} %collective-permute-done.32, f32[2048]{0:T(1024)S(1)} %bitcast.437), kind=kOutput, calls=%fused_computation.17 | convolution fusion | flops 269156352 | bytes 9052160 | tf_op jit(solution)/shard_map/dot_general | solution.py:146
  332.2 5.0 collective-permute-done.33
  337.1 6.0 %fusion.63 = f32[32,2048]{1,0:T(8,128)S(1)} fusion(bf16[2048,2048]{1,0:T(8,128)(2,1)} %bitcast.56, bf16[32,2048]{1,0:T(8,128)(2,1)S(1)} %collective-permute-done.33, bf16[32,2048]{1,0:T(8,128)(2,1)S(1)} %convolution_convert_fusion.11, bf16[32,2048]{1,0:T(8,128)(2,1)S(1)} %collective-permute-done.31, bf16[32,2048]{1,0:T(8,128)(2,1)S(1)} %fusion.10), kind=kOutput, calls=%fused_computation.206 | convolution fusion | flops 269418496 | bytes 9175040 | tf_op jit(solution)/shard_map/dot_general | solution.py:146
  355.4 4.9 fusion.7
  362.1 6.0 %convolution_convert_fusion.10 = bf16[32,2048]{1,0:T(8,128)(2,1)S(1)} fusion(bf16[2048,2048]{1,0:T(8,128)(2,1)} %bitcast.55, f32[32,2048]{1,0:T(8,128)S(1)} %fusion.7, f32[32,2048]{1,0:T(8,128)S(1)} %collective-permute-done.36, f32[2048]{0:T(1024)S(1)} %bitcast.438), kind=kOutput, calls=%fused_computation.16 | convolution fusion | flops 269156352 | bytes 9052160 | tf_op jit(solution)/shard_map/dot_general | solution.py:146
  373.6 6.0 %fusion.64 = f32[32,2048]{1,0:T(8,128)S(1)} fusion(bf16[2048,2048]{1,0:T(8,128)(2,1)} %bitcast.56, bf16[32,2048]{1,0:T(8,128)(2,1)S(1)} %collective-permute-done.37, bf16[32,2048]{1,0:T(8,128)(2,1)S(1)} %convolution_convert_fusion.10, bf16[32,2048]{1,0:T(8,128)(2,1)S(1)} %collective-permute-done.35, bf16[32,2048]{1,0:T(8,128)(2,1)S(1)} %fusion.11), kind=kOutput, calls=%fused_computation.207 | convolution fusion | flops 269418496 | bytes 9175040 | tf_op jit(solution)/shard_map/dot_general | solution.py:146
  381.2 5.0 convert_reduce_fusion.1
  387.2 13.0 %collective-permute-done.39 = f32[64,2048]{1,0:T(8,128)S(1)} collective-permute-done((f32[64,2048]{1,0:T(8,128)S(1)}, f32[64,2048]{1,0:T(8,128)S(1)}, u32[]{:S(2)}, u32[]{:S(2)}) %collective-permute-start.39) | collective-permute-done | bytes 524320 | tf_op jit(solution)/shard_map/ppermute | solution.py:23
  401.0 5.0 convert_reduce_fusion
  409.3 6.0 %fusion.132 = f32[64,2048]{1,0:T(8,128)S(1)} fusion(bf16[64,2048]{1,0:T(8,128)(2,1)S(1)} %get-tuple-element.54, bf16[2048,2048]{1,0:T(8,128)(2,1)} %bitcast.55), kind=kOutput, calls=%fused_computation.362 | convolution fusion | flops 536870912 | bytes 9175040 | tf_op jit(solution)/shard_map/dot_general | solution.py:146
  478.6 6.6 %collective-permute-done.60 = bf16[4,4,32,512]{3,2,1,0:T(8,128)(2,1)} collective-permute-done((bf16[4,4,32,512]{3,2,1,0:T(8,128)(2,1)}, bf16[4,4,32,512]{3,2,1,0:T(8,128)(2,1)}, u32[]{:S(2)}, u32[]{:S(2)}) %collective-permute-start.60) | collective-permute-done | bytes 524320 | tf_op jit(solution)/shard_map/ppermute | solution.py:23
  (354 shorter events, 259.7 us)
Async XLA Ops:
  5.8 14.3 %collective-permute-start = (bf16[64,2048]{1,0:T(8,128)(2,1)S(1)}, bf16[64,2048]{1,0:T(8,128)(2,1)S(1)}, u32[]{:S(2)}, u32[]{:S(2)}) collective-permute-start(bf16[64,2048]{1,0:T(8,128)(2,1)S(1)} %bitcast.440), channel_id=1, source_target_pairs={{0,1},{1,0},{2,3},{3,2},{4,5},{5,4},{6,7},{7,6},{8,9},{9,8},{10,11... | collective-permute-start | bytes 786440 | tf_op jit(solution)/shard_map/ppermute | solution.py:23
  17.2 43.1 %collective-permute-start.1 = (bf16[256,2048]{1,0:T(8,128)(2,1)S(1)}, bf16[256,2048]{1,0:T(8,128)(2,1)}, u32[]{:S(2)}, u32[]{:S(2)}) collective-permute-start(bf16[256,2048]{1,0:T(8,128)(2,1)S(1)} %bitcast.393), channel_id=1, source_target_pairs={{0,2},{2,0},{1,3},{3,1},{4,6},{6,4},{5,7},{7,5},{8,10},{10,8},{9,1... | collective-permute-start | bytes 3145736 | tf_op jit(solution)/shard_map/ppermute | solution.py:23
  20.2 28.9 %collective-permute-start.3 = (bf16[64,2048]{1,0:T(8,128)(2,1)S(1)}, bf16[64,2048]{1,0:T(8,128)(2,1)S(1)}, u32[]{:S(2)}, u32[]{:S(2)}) collective-permute-start(bf16[64,2048]{1,0:T(8,128)(2,1)S(1)} %broadcast_select_fusion.2), channel_id=1, source_target_pairs={{0,2},{2,0},{1,3},{3,1},{4,6},{6,4},{5,7},{7,5},{8,10},{10,8},{9,1... | collective-permute-start | bytes 786440 | tf_op jit(solution)/shard_map/ppermute | solution.py:23
  21.2 32.1 %collective-permute-start.2 = (bf16[64,2048]{1,0:T(8,128)(2,1)S(1)}, bf16[64,2048]{1,0:T(8,128)(2,1)S(1)}, u32[]{:S(2)}, u32[]{:S(2)}) collective-permute-start(bf16[64,2048]{1,0:T(8,128)(2,1)S(1)} %broadcast_select_fusion.2), channel_id=1, source_target_pairs={{0,4},{4,0},{8,12},{12,8},{1,5},{5,1},{9,13},{13,9},{2,6},{6,2},{1... | collective-permute-start | bytes 786440 | tf_op jit(solution)/shard_map/ppermute | solution.py:23
  53.3 19.3 %collective-permute-start.7 = (bf16[64,2048]{1,0:T(8,128)(2,1)S(1)}, bf16[64,2048]{1,0:T(8,128)(2,1)S(1)}, u32[]{:S(2)}, u32[]{:S(2)}) collective-permute-start(bf16[64,2048]{1,0:T(8,128)(2,1)S(1)} %collective-permute-done.3), channel_id=1, source_target_pairs={{0,4},{4,0},{8,12},{12,8},{1,5},{5,1},{9,13},{13,9},{2,6},{6,2},{1... | collective-permute-start | bytes 786440 | tf_op jit(solution)/shard_map/ppermute | solution.py:23
  53.4 16.2 %collective-permute-start.5 = (bf16[64,2048]{1,0:T(8,128)(2,1)S(1)}, bf16[64,2048]{1,0:T(8,128)(2,1)}, u32[]{:S(2)}, u32[]{:S(2)}) collective-permute-start(bf16[64,2048]{1,0:T(8,128)(2,1)S(1)} %collective-permute-done.2), channel_id=1, source_target_pairs={{0,12},{4,8},{8,4},{12,0},{1,13},{5,9},{9,5},{13,1},{2,14},{6,10},... | collective-permute-start | bytes 786440 | tf_op jit(solution)/shard_map/ppermute | solution.py:23
  60.3 115.7 %collective-permute-start.11 = (bf16[256,2048]{1,0:T(8,128)(2,1)S(1)}, bf16[256,2048]{1,0:T(8,128)(2,1)}, u32[]{:S(2)}, u32[]{:S(2)}) collective-permute-start(bf16[256,2048]{1,0:T(8,128)(2,1)S(1)} %bitcast.394), channel_id=1, source_target_pairs={{0,4},{4,0},{8,12},{12,8},{1,5},{5,1},{9,13},{13,9},{2,6},{6,2},{1... | collective-permute-start | bytes 3145736 | tf_op jit(solution)/shard_map/ppermute | solution.py:23
  65.9 112.4 %collective-permute-start.12 = (bf16[256,2048]{1,0:T(8,128)(2,1)}, bf16[256,2048]{1,0:T(8,128)(2,1)}, u32[]{:S(2)}, u32[]{:S(2)}) collective-permute-start(bf16[256,2048]{1,0:T(8,128)(2,1)} %collective-permute-done.1), channel_id=1, source_target_pairs={{0,4},{4,0},{8,12},{12,8},{1,5},{5,1},{9,13},{13,9},{2,6},{6,2},{1... | collective-permute-start | bytes 3145736 | tf_op jit(solution)/shard_map/ppermute | solution.py:23
  69.6 129.8 %collective-permute-start.14 = (bf16[256,2048]{1,0:T(8,128)(2,1)}, bf16[256,2048]{1,0:T(8,128)(2,1)}, u32[]{:S(2)}, u32[]{:S(2)}) collective-permute-start(bf16[256,2048]{1,0:T(8,128)(2,1)} %collective-permute-done.1), channel_id=1, source_target_pairs={{0,12},{4,8},{8,4},{12,0},{1,13},{5,9},{9,5},{13,1},{2,14},{6,10},... | collective-permute-start | bytes 3145736 | tf_op jit(solution)/shard_map/ppermute | solution.py:23
  72.5 146.0 %collective-permute-start.16 = (bf16[256,2048]{1,0:T(8,128)(2,1)S(1)}, bf16[256,2048]{1,0:T(8,128)(2,1)}, u32[]{:S(2)}, u32[]{:S(2)}) collective-permute-start(bf16[256,2048]{1,0:T(8,128)(2,1)S(1)} %bitcast.396), channel_id=1, source_target_pairs={{0,12},{4,8},{8,4},{12,0},{1,13},{5,9},{9,5},{13,1},{2,14},{6,10},... | collective-permute-start | bytes 3145736 | tf_op jit(solution)/shard_map/ppermute | solution.py:23
  73.7 49.9 %all-to-all-start.1 = ((f32[8,5,16,256]{3,2,1,0:T(8,128)}), f32[8,5,16,256]{3,2,1,0:T(8,128)S(1)}, u32[]{:S(2)}, u32[]{:S(2)}) async-start(f32[8,5,16,256]{3,2,1,0:T(8,128)} %copy.162), calls=%async_computation.1 | async-start | bytes 1310720 | tf_op jit(solution)/shard_map/all_to_all | solution.py:107
  84.0 40.3 %collective-permute-start.18 = (bf16[256,2048]{1,0:T(8,128)(2,1)}, bf16[256,2048]{1,0:T(8,128)(2,1)}, u32[]{:S(2)}, u32[]{:S(2)}) collective-permute-start(bf16[256,2048]{1,0:T(8,128)(2,1)} %constant_dynamic-update-slice_fusion), channel_id=1, source_target_pairs={{0,32},{32,0},{64,96},{96,64},{1,33},{33,1},{65,97},{97,65},{2,34}... | collective-permute-start | bytes 3145736 | tf_op jit(solution)/shard_map/ppermute | solution.py:23
  124.3 22.5 %collective-permute-start.19 = (bf16[256,2048]{1,0:T(8,128)(2,1)}, bf16[256,2048]{1,0:T(8,128)(2,1)S(1)}, u32[]{:S(2)}, u32[]{:S(2)}) collective-permute-start(bf16[256,2048]{1,0:T(8,128)(2,1)} %copy-done.16), channel_id=1, source_target_pairs={{0,32},{32,0},{64,96},{96,64},{1,33},{33,1},{65,97},{97,65},{2,34}... | collective-permute-start | bytes 3145736 | tf_op jit(solution)/shard_map/ppermute | solution.py:23
  146.8 23.3 %collective-permute-start.20 = (bf16[256,2048]{1,0:T(8,128)(2,1)}, bf16[256,2048]{1,0:T(8,128)(2,1)S(1)}, u32[]{:S(2)}, u32[]{:S(2)}) collective-permute-start(bf16[256,2048]{1,0:T(8,128)(2,1)} %constant_dynamic-update-slice_fusion), channel_id=1, source_target_pairs={{0,96},{32,64},{64,32},{96,0},{1,97},{33,65},{65,33},{97,1},{2,98}... | collective-permute-start | bytes 3145736 | tf_op jit(solution)/shard_map/ppermute | solution.py:23
  170.1 23.3 %collective-permute-start.21 = (bf16[256,2048]{1,0:T(8,128)(2,1)}, bf16[256,2048]{1,0:T(8,128)(2,1)S(1)}, u32[]{:S(2)}, u32[]{:S(2)}) collective-permute-start(bf16[256,2048]{1,0:T(8,128)(2,1)} %copy-done.16), channel_id=1, source_target_pairs={{0,96},{32,64},{64,32},{96,0},{1,97},{33,65},{65,33},{97,1},{2,98}... | collective-permute-start | bytes 3145736 | tf_op jit(solution)/shard_map/ppermute | solution.py:23
  176.1 23.5 %collective-permute-start.10 = (f32[5,16,2048]{2,1,0:T(8,128)S(1)}, f32[5,16,2048]{2,1,0:T(8,128)S(1)}, u32[]{:S(2)}, u32[]{:S(2)}) collective-permute-start(f32[5,16,2048]{2,1,0:T(8,128)S(1)} %reshape.200), channel_id=1, source_target_pairs={{0,16},{16,0},{1,17},{17,1},{2,18},{18,2},{3,19},{19,3},{4,20},{20... | collective-permute-start | bytes 1966088 | tf_op jit(solution)/shard_map/ppermute | solution.py:23
  178.4 27.0 %collective-permute-start.13 = (bf16[256,2048]{1,0:T(8,128)(2,1)}, bf16[256,2048]{1,0:T(8,128)(2,1)S(1)}, u32[]{:S(2)}, u32[]{:S(2)}) collective-permute-start(bf16[256,2048]{1,0:T(8,128)(2,1)} %collective-permute-done.11), channel_id=1, source_target_pairs={{0,12},{4,8},{8,4},{12,0},{1,13},{5,9},{9,5},{13,1},{2,14},{6,10},... | collective-permute-start | bytes 3145736 | tf_op jit(solution)/shard_map/ppermute | solution.py:23
  193.5 35.4 %collective-permute-start.22 = (bf16[256,2048]{1,0:T(8,128)(2,1)}, bf16[256,2048]{1,0:T(8,128)(2,1)S(1)}, u32[]{:S(2)}, u32[]{:S(2)}) collective-permute-start(bf16[256,2048]{1,0:T(8,128)(2,1)} %collective-permute-done.18), channel_id=1, source_target_pairs={{0,96},{32,64},{64,32},{96,0},{1,97},{33,65},{65,33},{97,1},{2,98}... | collective-permute-start | bytes 3145736 | tf_op jit(solution)/shard_map/ppermute | solution.py:23
  199.4 32.4 %collective-permute-start.23 = (bf16[256,2048]{1,0:T(8,128)(2,1)S(1)}, bf16[256,2048]{1,0:T(8,128)(2,1)S(1)}, u32[]{:S(2)}, u32[]{:S(2)}) collective-permute-start(bf16[256,2048]{1,0:T(8,128)(2,1)S(1)} %collective-permute-done.21), channel_id=1, source_target_pairs={{0,32},{32,0},{64,96},{96,64},{1,33},{33,1},{65,97},{97,65},{2,34}... | collective-permute-start | bytes 3145736 | tf_op jit(solution)/shard_map/ppermute | solution.py:23
  199.5 18.0 %collective-permute-start.15 = (bf16[256,2048]{1,0:T(8,128)(2,1)}, bf16[256,2048]{1,0:T(8,128)(2,1)S(1)}, u32[]{:S(2)}, u32[]{:S(2)}) collective-permute-start(bf16[256,2048]{1,0:T(8,128)(2,1)} %collective-permute-done.14), channel_id=1, source_target_pairs={{0,4},{4,0},{8,12},{12,8},{1,5},{5,1},{9,13},{13,9},{2,6},{6,2},{1... | collective-permute-start | bytes 3145736 | tf_op jit(solution)/shard_map/ppermute | solution.py:23
  386.2 14.0 %collective-permute-start.39 = (f32[64,2048]{1,0:T(8,128)S(1)}, f32[64,2048]{1,0:T(8,128)S(1)}, u32[]{:S(2)}, u32[]{:S(2)}) collective-permute-start(f32[64,2048]{1,0:T(8,128)S(1)} %convert_reduce_fusion.1), channel_id=1, source_target_pairs={{0,1},{1,0},{2,3},{3,2},{4,5},{5,4},{6,7},{7,6},{8,9},{9,8},{10,11... | collective-permute-start | bytes 1572872 | tf_op jit(solution)/shard_map/ppermute | solution.py:23
  415.3 15.3 %collective-permute-start.50 = (f32[64,2048]{1,0:T(8,128)S(1)}, f32[64,2048]{1,0:T(8,128)}, u32[]{:S(2)}, u32[]{:S(2)}) collective-permute-start(f32[64,2048]{1,0:T(8,128)S(1)} %fusion.132), channel_id=1, source_target_pairs={{0,1},{1,0},{2,3},{3,2},{4,5},{5,4},{6,7},{7,6},{8,9},{9,8},{10,11... | collective-permute-start | bytes 1572872 | tf_op jit(solution)/shard_map/ppermute | solution.py:23
  426.1 18.9 %collective-permute-start.47 = (bf16[4,2,32,512]{3,2,1,0:T(8,128)(2,1)}, bf16[4,2,32,512]{3,2,1,0:T(8,128)(2,1)S(1)}, u32[]{:S(2)}, u32[]{:S(2)}) collective-permute-start(bf16[4,2,32,512]{3,2,1,0:T(8,128)(2,1)} %get-tuple-element.80), channel_id=1, source_target_pairs={{0,96},{32,64},{64,32},{96,0},{1,97},{33,65},{65,33},{97,1},{2,98}... | collective-permute-start | bytes 786440 | tf_op jit(solution)/shard_map/ppermute | solution.py:23
  426.4 19.0 %collective-permute-start.46 = (bf16[4,2,32,512]{3,2,1,0:T(8,128)(2,1)}, bf16[4,2,32,512]{3,2,1,0:T(8,128)(2,1)S(1)}, u32[]{:S(2)}, u32[]{:S(2)}) collective-permute-start(bf16[4,2,32,512]{3,2,1,0:T(8,128)(2,1)} %get-tuple-element.80), channel_id=1, source_target_pairs={{0,64},{32,96},{64,0},{96,32},{1,65},{33,97},{65,1},{97,33},{2,66}... | collective-permute-start | bytes 786440 | tf_op jit(solution)/shard_map/ppermute | solution.py:23
  429.8 17.2 %collective-permute-start.45 = (bf16[4,2,32,512]{3,2,1,0:T(8,128)(2,1)}, bf16[4,2,32,512]{3,2,1,0:T(8,128)(2,1)S(1)}, u32[]{:S(2)}, u32[]{:S(2)}) collective-permute-start(bf16[4,2,32,512]{3,2,1,0:T(8,128)(2,1)} %get-tuple-element.80), channel_id=1, source_target_pairs={{0,32},{32,0},{64,96},{96,64},{1,33},{33,1},{65,97},{97,65},{2,34}... | collective-permute-start | bytes 786440 | tf_op jit(solution)/shard_map/ppermute | solution.py:23
  447.8 20.8 %collective-permute-start.48 = (bf16[4,4,2,32,512]{4,3,2,1,0:T(8,128)(2,1)S(1)}, bf16[4,4,2,32,512]{4,3,2,1,0:T(8,128)(2,1)S(1)}, u32[]{:S(2)}, u32[]{:S(2)}) collective-permute-start(bf16[4,4,2,32,512]{4,3,2,1,0:T(8,128)(2,1)S(1)} %pad_maximum_fusion.3), channel_id=1, source_target_pairs={{0,16},{16,0},{1,17},{17,1},{2,18},{18,2},{3,19},{19,3},{4,20},{20... | collective-permute-start | bytes 3145736 | tf_op jit(solution)/shard_map/ppermute | solution.py:23
  458.0 18.8 %collective-permute-start.59 = (bf16[4,4,32,512]{3,2,1,0:T(8,128)(2,1)}, bf16[4,4,32,512]{3,2,1,0:T(8,128)(2,1)}, u32[]{:S(2)}, u32[]{:S(2)}) collective-permute-start(bf16[4,4,32,512]{3,2,1,0:T(8,128)(2,1)} %pad_maximum_fusion.7), channel_id=1, source_target_pairs={{0,2},{1,3},{2,0},{3,1},{4,6},{5,7},{6,4},{7,5},{8,10},{9,11},{10,... | collective-permute-start | bytes 1572872 | tf_op jit(solution)/shard_map/ppermute | solution.py:23
  461.8 23.5 %collective-permute-start.60 = (bf16[4,4,32,512]{3,2,1,0:T(8,128)(2,1)}, bf16[4,4,32,512]{3,2,1,0:T(8,128)(2,1)}, u32[]{:S(2)}, u32[]{:S(2)}) collective-permute-start(bf16[4,4,32,512]{3,2,1,0:T(8,128)(2,1)} %pad_maximum_fusion.7), channel_id=1, source_target_pairs={{0,3},{1,2},{2,1},{3,0},{4,7},{5,6},{6,5},{7,4},{8,11},{9,10},{10,... | collective-permute-start | bytes 1572872 | tf_op jit(solution)/shard_map/ppermute | solution.py:23
  462.7 24.0 %collective-permute-start.58 = (bf16[4,4,32,512]{3,2,1,0:T(8,128)(2,1)}, bf16[4,4,32,512]{3,2,1,0:T(8,128)(2,1)}, u32[]{:S(2)}, u32[]{:S(2)}) collective-permute-start(bf16[4,4,32,512]{3,2,1,0:T(8,128)(2,1)} %pad_maximum_fusion.7), channel_id=1, source_target_pairs={{0,1},{1,0},{2,3},{3,2},{4,5},{5,4},{6,7},{7,6},{8,9},{9,8},{10,11... | collective-permute-start | bytes 1572872 | tf_op jit(solution)/shard_map/ppermute | solution.py:23
  465.6 25.2 %collective-permute-start.70 = (bf16[2,4,2,32,512]{4,3,2,1,0:T(8,128)(2,1)}, bf16[2,4,2,32,512]{4,3,2,1,0:T(8,128)(2,1)}, u32[]{:S(2)}, u32[]{:S(2)}) collective-permute-start(bf16[2,4,2,32,512]{4,3,2,1,0:T(8,128)(2,1)} %get-tuple-element.66), channel_id=1, source_target_pairs={{0,12},{4,8},{8,4},{12,0},{1,13},{5,9},{9,5},{13,1},{2,14},{6,10},... | collective-permute-start | bytes 1572872 | tf_op jit(solution)/shard_map/ppermute | solution.py:23
  468.6 22.3 %collective-permute-start.69 = (bf16[2,4,2,32,512]{4,3,2,1,0:T(8,128)(2,1)}, bf16[2,4,2,32,512]{4,3,2,1,0:T(8,128)(2,1)}, u32[]{:S(2)}, u32[]{:S(2)}) collective-permute-start(bf16[2,4,2,32,512]{4,3,2,1,0:T(8,128)(2,1)} %get-tuple-element.66), channel_id=1, source_target_pairs={{0,8},{4,12},{8,0},{12,4},{1,9},{5,13},{9,1},{13,5},{2,10},{6,14},... | collective-permute-start | bytes 1572872 | tf_op jit(solution)/shard_map/ppermute | solution.py:23
  476.8 14.6 %collective-permute-start.68 = (bf16[2,4,2,32,512]{4,3,2,1,0:T(8,128)(2,1)}, bf16[2,4,2,32,512]{4,3,2,1,0:T(8,128)(2,1)S(1)}, u32[]{:S(2)}, u32[]{:S(2)}) collective-permute-start(bf16[2,4,2,32,512]{4,3,2,1,0:T(8,128)(2,1)} %get-tuple-element.66), channel_id=1, source_target_pairs={{0,4},{4,0},{8,12},{12,8},{1,5},{5,1},{9,13},{13,9},{2,6},{6,2},{1... | collective-permute-start | bytes 1572872 | tf_op jit(solution)/shard_map/ppermute | solution.py:23
  (70 other events, 557.9 us)
